TPU v7x, 32 devices: a whole 2x2x4 slice. The times are simulated.
32 devices in a mesh: dp: 4 (over z), ctx: 2 (over x), fsdp: 4 (over y, core).
Axes of the slice: x: 2, y: 2, z: 4, core: 2. Of those that a mesh axis runs over, the one named last changes fastest.
Arguments:
- tokens: bfloat16 [32, 1024, 576], P(('dp', 'fsdp'), 'ctx'), may hold values from -6 to 6
- norm1_gain: bfloat16 [576], P('fsdp'), may hold values from 0.5 to 1.5
- w_query: bfloat16 [576, 576], P('fsdp'), may hold values from -0.25 to 0.25
- w_key: bfloat16 [576, 192], P('fsdp'), may hold values from -0.25 to 0.25
- w_value: bfloat16 [576, 192], P('fsdp'), may hold values from -0.25 to 0.25
- w_out: bfloat16 [576, 576], P('fsdp'), may hold values from -2 to 2
- norm2_gain: bfloat16 [576], P('fsdp'), may hold values from 0.5 to 1.5
- w_gate: bfloat16 [576, 1536], P('fsdp'), may hold values from -0.25 to 0.25
- w_up: bfloat16 [576, 1536], P('fsdp'), may hold values from -0.25 to 0.25
- w_down: bfloat16 [1536, 576], P('fsdp'), may hold values from -0.15625 to 0.15625
- out_grad: bfloat16 [32, 1024, 576], P(('dp', 'fsdp'), 'ctx'), may hold values from -6 to 6
Outputs:
- output: bfloat16 [32, 1024, 576], P(('dp', 'fsdp'), 'ctx')
- input_grad: float32 [32, 1024, 576], P(('dp', 'fsdp'), 'ctx')
- norm1_gain_grad: float32 [576], P('fsdp')
- w_query_grad: float32 [576, 576], P('fsdp')
- w_key_grad: float32 [576, 192], P('fsdp')
- w_value_grad: float32 [576, 192], P('fsdp')
- w_out_grad: float32 [576, 576], P('fsdp')
- norm2_gain_grad: float32 [576], P('fsdp')
- w_gate_grad: float32 [576, 1536], P('fsdp')
- w_up_grad: float32 [576, 1536], P('fsdp')
- w_down_grad: float32 [1536, 576], P('fsdp')
All inputs are finite; a program needn't handle non-finite values.
Results may differ from a plain program's by a relative error of at most 0.03.
Values may be sent and summed in bfloat16 or wider, within the bound.
No kernel may reach another device: no remote copies, remote signals or barrier semaphores. Data moves between devices by JAX's collectives and lax.ppermute only.
A program may use at most 192 MiB of HBM per device.

v0:
```python
import math

import jax
import jax.numpy as jnp
from jax import lax
from jax.sharding import PartitionSpec as P

QUERY_HEADS = 9
KEY_VALUE_HEADS = 3
HEAD_SIZE = 64


EPSILON = 1e-05
ROPE_THETA = 100000.0
MASKED = -1e30


def rope_tables(positions, head_width):
    half_size = head_width // 2
    inverse = jnp.exp(
        jnp.arange(half_size, dtype=jnp.float32) * (-2.0 * math.log(ROPE_THETA) / head_width)
    )
    angle = positions.astype(jnp.float32)[:, None] * inverse[None, :]
    return (jnp.cos(angle), jnp.sin(angle))


def rotary_apply(tensor, cosine_table, sine_table):
    half_size = tensor.shape[-1] // 2
    first_half = tensor[..., :half_size]
    second_half = tensor[..., half_size:]
    cosine_table = cosine_table[None, :, None, :]
    sine_table = sine_table[None, :, None, :]
    return jnp.concatenate(
        [
            first_half * cosine_table - second_half * sine_table,
            second_half * cosine_table + first_half * sine_table,
        ],
        -1,
    )


def rotate_back(tensor, cosine_table, sine_table):
    half_size = tensor.shape[-1] // 2
    first_half = tensor[..., :half_size]
    second_half = tensor[..., half_size:]
    cosine_table = cosine_table[None, :, None, :]
    sine_table = sine_table[None, :, None, :]
    return jnp.concatenate(
        [
            first_half * cosine_table + second_half * sine_table,
            second_half * cosine_table - first_half * sine_table,
        ],
        -1,
    )


def rms_scale(tensor):
    return lax.rsqrt(jnp.mean(tensor * tensor, axis=-1, keepdims=True) + EPSILON)


def block_scores(query_block, key_block, query_pos, key_pos):
    scores = (
        jnp.einsum("gqhrd,gkhd->ghrqk", query_block, key_block, preferred_element_type=jnp.float32)
        * 0.125
    )
    visible = key_pos[None, :] <= query_pos[:, None]
    return jnp.where(visible, scores, MASKED)


def local(
    tokens, norm1_gain, w_query, w_key, w_value, w_out, norm2_gain, w_gate, w_up, w_down, out_grad
):
    gain1, wq_full, wk_full, wv_full, wo_full, gain2, wg_full, wu_full, wd_full = (
        lax.all_gather(norm1_gain, "fsdp", axis=0, tiled=True),
        lax.all_gather(w_query, "fsdp", axis=0, tiled=True),
        lax.all_gather(w_key, "fsdp", axis=0, tiled=True),
        lax.all_gather(w_value, "fsdp", axis=0, tiled=True),
        lax.all_gather(w_out, "fsdp", axis=0, tiled=True),
        lax.all_gather(norm2_gain, "fsdp", axis=0, tiled=True),
        lax.all_gather(w_gate, "fsdp", axis=0, tiled=True),
        lax.all_gather(w_up, "fsdp", axis=0, tiled=True),
        lax.all_gather(w_down, "fsdp", axis=0, tiled=True),
    )
    query_group_count, local_row_count, model_width = tokens.shape
    repeat_heads = QUERY_HEADS // KEY_VALUE_HEADS
    head_width = HEAD_SIZE
    key_value_width = KEY_VALUE_HEADS * HEAD_SIZE
    query_width = QUERY_HEADS * HEAD_SIZE
    first_row = lax.axis_index("ctx") * local_row_count
    last_row = first_row + local_row_count - 1
    positions = first_row + jnp.arange(local_row_count, dtype=jnp.int32)
    cosine_table, sine_table = rope_tables(positions, head_width)
    gain1f = gain1.astype(jnp.float32)
    gain2f = gain2.astype(jnp.float32)
    inputs = tokens.astype(jnp.float32)
    scale1 = rms_scale(inputs)
    normed1 = (inputs * scale1 * gain1f).astype(jnp.bfloat16)
    query_before_rotation = jnp.einsum(
        "gsd,de->gse", normed1, wq_full, preferred_element_type=jnp.float32
    )
    key_before_rotation = jnp.einsum(
        "gsd,de->gse", normed1, wk_full, preferred_element_type=jnp.float32
    )
    value_projected = jnp.einsum(
        "gsd,de->gse", normed1, wv_full, preferred_element_type=jnp.float32
    )
    query_matrix = rotary_apply(
        query_before_rotation.reshape(query_group_count, local_row_count, QUERY_HEADS, head_width),
        cosine_table,
        sine_table,
    ).astype(jnp.bfloat16)
    query_matrix = query_matrix.reshape(
        query_group_count, local_row_count, KEY_VALUE_HEADS, repeat_heads, head_width
    )
    key_local = rotary_apply(
        key_before_rotation.reshape(
            query_group_count, local_row_count, KEY_VALUE_HEADS, head_width
        ),
        cosine_table,
        sine_table,
    ).astype(jnp.bfloat16)
    local_value_rows = value_projected.astype(jnp.bfloat16)
    collected_keys, collected_values = (
        lax.all_gather(
            key_local.reshape(query_group_count, local_row_count, key_value_width),
            "ctx",
            axis=1,
            tiled=True,
        ),
        lax.all_gather(local_value_rows, "ctx", axis=1, tiled=True),
    )
    sequence_length = collected_keys.shape[1]
    every_key_row = collected_keys.reshape(
        query_group_count, sequence_length, KEY_VALUE_HEADS, head_width
    )
    every_value_row = collected_values.reshape(
        query_group_count, sequence_length, KEY_VALUE_HEADS, head_width
    )
    local_value_rows = local_value_rows.reshape(
        query_group_count, local_row_count, KEY_VALUE_HEADS, head_width
    )
    key_span = min(sequence_length, 512)
    block_total = last_row // key_span + 1

    def key_slices(step_index):
        first_key = step_index * key_span
        key_block = lax.dynamic_slice_in_dim(every_key_row, first_key, key_span, 1)
        value_block = lax.dynamic_slice_in_dim(every_value_row, first_key, key_span, 1)
        key_pos = first_key + jnp.arange(key_span, dtype=jnp.int32)
        return (key_block, value_block, key_pos)

    def stats_step(step_index, running):
        row_max, row_sum = running
        key_block, value_block, key_pos = key_slices(step_index)
        scores = block_scores(query_matrix, key_block, positions, key_pos)
        new_max = jnp.maximum(row_max, jnp.max(scores, axis=-1))
        row_sum = row_sum * jnp.exp(row_max - new_max) + jnp.sum(
            jnp.exp(scores - new_max[..., None]), axis=-1
        )
        return (new_max, row_sum)

    statistics_shape = (query_group_count, KEY_VALUE_HEADS, repeat_heads, local_row_count)
    row_max, row_sum = lax.fori_loop(
        0,
        block_total,
        stats_step,
        (jnp.full(statistics_shape, MASKED, jnp.float32), jnp.zeros(statistics_shape, jnp.float32)),
    )
    log_total = row_max + jnp.log(row_sum)

    def mix_step(step_index, running):
        key_block, value_block, key_pos = key_slices(step_index)
        scores = block_scores(query_matrix, key_block, positions, key_pos)
        probs = jnp.exp(scores - log_total[..., None]).astype(jnp.bfloat16)
        return running + jnp.einsum(
            "ghrqk,gkhd->gqhrd", probs, value_block, preferred_element_type=jnp.float32
        )

    attended_full = lax.fori_loop(
        0,
        block_total,
        mix_step,
        jnp.zeros(
            (query_group_count, local_row_count, KEY_VALUE_HEADS, repeat_heads, head_width),
            jnp.float32,
        ),
    )
    attended = attended_full.astype(jnp.bfloat16).reshape(
        query_group_count, local_row_count, query_width
    )
    branch = jnp.einsum("gse,ed->gsd", attended, wo_full, preferred_element_type=jnp.float32)
    middle = inputs + branch
    scale2 = rms_scale(middle)
    normed2 = (middle * scale2 * gain2f).astype(jnp.bfloat16)
    gate_act = jnp.einsum("gsd,df->gsf", normed2, wg_full, preferred_element_type=jnp.float32)
    up_act = jnp.einsum("gsd,df->gsf", normed2, wu_full, preferred_element_type=jnp.float32)
    gate_sig = jax.nn.sigmoid(gate_act)
    gate_silu = gate_act * gate_sig
    hidden = (gate_silu * up_act).astype(jnp.bfloat16)
    mlp_out = jnp.einsum("gsf,fd->gsd", hidden, wd_full, preferred_element_type=jnp.float32)
    output = (middle + mlp_out).astype(jnp.bfloat16)
    out_float = out_grad.astype(jnp.float32)
    grad_down = jnp.einsum("gsf,gsd->fd", hidden, out_grad, preferred_element_type=jnp.float32)
    hidden_grad = jnp.einsum("gsd,fd->gsf", out_grad, wd_full, preferred_element_type=jnp.float32)
    gate_grad = (hidden_grad * up_act * gate_sig * (1.0 + gate_act * (1.0 - gate_sig))).astype(
        jnp.bfloat16
    )
    up_grad = (hidden_grad * gate_silu).astype(jnp.bfloat16)
    grad_gate = jnp.einsum("gsd,gsf->df", normed2, gate_grad, preferred_element_type=jnp.float32)
    grad_up = jnp.einsum("gsd,gsf->df", normed2, up_grad, preferred_element_type=jnp.float32)
    normed2_grad = jnp.einsum("gsf,df->gsd", gate_grad, wg_full, preferred_element_type=jnp.float32)
    normed2_grad = normed2_grad + jnp.einsum(
        "gsf,df->gsd", up_grad, wu_full, preferred_element_type=jnp.float32
    )
    grad_gain2 = jnp.sum(normed2_grad * middle * scale2, axis=(0, 1))
    scaled2 = gain2f * normed2_grad
    middle_grad = (
        out_float
        + scale2 * scaled2
        - middle * scale2**3 * jnp.mean(scaled2 * middle, axis=-1, keepdims=True)
    )
    branch_grad = middle_grad.astype(jnp.bfloat16)
    grad_out = jnp.einsum("gse,gsd->ed", attended, branch_grad, preferred_element_type=jnp.float32)
    attended_output_gradient = jnp.einsum(
        "gsd,ed->gse", branch_grad, wo_full, preferred_element_type=jnp.float32
    ).astype(jnp.bfloat16)
    attention_gradient = attended_output_gradient.reshape(
        query_group_count, local_row_count, KEY_VALUE_HEADS, repeat_heads, head_width
    )
    delta = jnp.sum(attention_gradient.astype(jnp.float32) * attended_full, axis=-1).transpose(
        0, 2, 3, 1
    )

    def query_grad_step(step_index, running):
        key_block, value_block, key_pos = key_slices(step_index)
        scores = block_scores(query_matrix, key_block, positions, key_pos)
        probs = jnp.exp(scores - log_total[..., None])
        dprob = jnp.einsum(
            "gqhrd,gkhd->ghrqk", attention_gradient, value_block, preferred_element_type=jnp.float32
        )
        score_grad = (probs * (dprob - delta[..., None])).astype(jnp.bfloat16)
        return running + jnp.einsum(
            "ghrqk,gkhd->gqhrd", score_grad, key_block, preferred_element_type=jnp.float32
        )

    query_grad = (
        lax.fori_loop(
            0,
            block_total,
            query_grad_step,
            jnp.zeros(
                (query_group_count, local_row_count, KEY_VALUE_HEADS, repeat_heads, head_width),
                jnp.float32,
            ),
        )
        * 0.125
    )
    row_total = local_row_count * lax.axis_size("ctx")
    term_span = math.gcd(row_total, key_span)

    def key_block_term(step_index):
        first_key = step_index * term_span
        key_block = lax.dynamic_slice_in_dim(every_key_row, first_key, term_span, 1)
        value_block = lax.dynamic_slice_in_dim(every_value_row, first_key, term_span, 1)
        key_pos = first_key + jnp.arange(term_span, dtype=jnp.int32)

        def compute_term(unused):
            scores = block_scores(query_matrix, key_block, positions, key_pos)
            probs = jnp.exp(scores - log_total[..., None])
            dprob = jnp.einsum(
                "gqhrd,gkhd->ghrqk",
                attention_gradient,
                value_block,
                preferred_element_type=jnp.float32,
            )
            score_grad = (probs * (dprob - delta[..., None])).astype(jnp.bfloat16)
            key_term = (
                jnp.einsum(
                    "ghrqk,gqhrd->kghd",
                    score_grad,
                    query_matrix,
                    preferred_element_type=jnp.float32,
                )
                * 0.125
            )
            value_term = jnp.einsum(
                "ghrqk,gqhrd->kghd",
                probs.astype(jnp.bfloat16),
                attention_gradient,
                preferred_element_type=jnp.float32,
            )
            return jnp.concatenate(
                [
                    key_term.reshape(term_span, query_group_count, key_value_width),
                    value_term.reshape(term_span, query_group_count, key_value_width),
                ],
                -1,
            )

        def empty_term(unused):
            return jnp.zeros((term_span, query_group_count, 2 * key_value_width), jnp.float32)

        return lax.cond(first_key <= last_row, compute_term, empty_term, 0)

    terms = lax.map(key_block_term, jnp.arange(row_total // term_span, dtype=jnp.int32))
    paired_gradients = (
        lax.psum_scatter(
            terms.reshape(row_total, query_group_count, 2 * key_value_width).astype(jnp.bfloat16),
            "ctx",
            scatter_dimension=0,
            tiled=True,
        )
        .astype(jnp.float32)
        .transpose(1, 0, 2)
    )
    key_gradient = paired_gradients[..., :key_value_width].reshape(
        query_group_count, local_row_count, KEY_VALUE_HEADS, head_width
    )
    value_gradient = paired_gradients[..., key_value_width:].reshape(
        query_group_count, local_row_count, KEY_VALUE_HEADS, head_width
    )
    query_pre_grad = rotate_back(
        query_grad.reshape(query_group_count, local_row_count, QUERY_HEADS, head_width),
        cosine_table,
        sine_table,
    )
    query_pre_grad = query_pre_grad.astype(jnp.bfloat16).reshape(
        query_group_count, local_row_count, query_width
    )
    key_pre_grad = (
        rotate_back(key_gradient, cosine_table, sine_table)
        .astype(jnp.bfloat16)
        .reshape(query_group_count, local_row_count, key_value_width)
    )
    value_pre_grad = value_gradient.astype(jnp.bfloat16).reshape(
        query_group_count, local_row_count, key_value_width
    )
    grad_query = jnp.einsum(
        "gsd,gse->de", normed1, query_pre_grad, preferred_element_type=jnp.float32
    )
    grad_key = jnp.einsum("gsd,gse->de", normed1, key_pre_grad, preferred_element_type=jnp.float32)
    grad_value = jnp.einsum(
        "gsd,gse->de", normed1, value_pre_grad, preferred_element_type=jnp.float32
    )
    normed1_grad = jnp.einsum(
        "gse,de->gsd", query_pre_grad, wq_full, preferred_element_type=jnp.float32
    )
    normed1_grad = normed1_grad + jnp.einsum(
        "gse,de->gsd", key_pre_grad, wk_full, preferred_element_type=jnp.float32
    )
    normed1_grad = normed1_grad + jnp.einsum(
        "gse,de->gsd", value_pre_grad, wv_full, preferred_element_type=jnp.float32
    )
    grad_gain1 = jnp.sum(normed1_grad * inputs * scale1, axis=(0, 1))
    scaled1 = gain1f * normed1_grad
    input_grad = (
        middle_grad
        + scale1 * scaled1
        - inputs * scale1**3 * jnp.mean(scaled1 * inputs, axis=-1, keepdims=True)
    )
    totals = lax.psum(
        (
            grad_gain1,
            grad_query,
            grad_key,
            grad_value,
            grad_out,
            grad_gain2,
            grad_gate,
            grad_up,
            grad_down,
        ),
        ("dp", "ctx", "fsdp"),
    )
    owner = lax.axis_index("fsdp")
    shards = (norm1_gain, w_query, w_key, w_value, w_out, norm2_gain, w_gate, w_up, w_down)
    shares = tuple(
        (
            lax.dynamic_slice_in_dim(summed, owner * shard.shape[0], shard.shape[0], 0)
            for summed, shard in zip(totals, shards)
        )
    )
    return (
        output,
        input_grad,
        shares[0],
        shares[1],
        shares[2],
        shares[3],
        shares[4],
        shares[5],
        shares[6],
        shares[7],
        shares[8],
    )


def solution(mesh):
    return jax.shard_map(
        local,
        mesh=mesh,
        in_specs=(
            P(("dp", "fsdp"), "ctx", None),
            P("fsdp"),
            P("fsdp", None),
            P("fsdp", None),
            P("fsdp", None),
            P("fsdp", None),
            P("fsdp"),
            P("fsdp", None),
            P("fsdp", None),
            P("fsdp", None),
            P(("dp", "fsdp"), "ctx", None),
        ),
        out_specs=(
            P(("dp", "fsdp"), "ctx", None),
            P(("dp", "fsdp"), "ctx", None),
            P("fsdp"),
            P("fsdp", None),
            P("fsdp", None),
            P("fsdp", None),
            P("fsdp", None),
            P("fsdp"),
            P("fsdp", None),
            P("fsdp", None),
            P("fsdp", None),
        ),
        check_vma=False,
    )
```

profile of v0, /device:TPU:0, one launch (start us, length us, event | category | flops | bytes accessed | tf_op | source)
XLA Modules:
  0.0 639.1 jit_solution(4681477747921021770)
XLA Ops:
  9.5 7.6 %all_gather.34 = bf16[576,192]{1,0:T(8,128)(2,1)S(1)} all-gather(bf16[144,192]{1,0:T(8,128)(2,1)} %param.25), channel_id=1, replica_groups=mesh['dp'=4,'ctx'=2,'fsdp'=4] {'fsdp'}, dimensions={0}, use_global_device_ids=true | all-gather | bytes 276480 | tf_op jit(solution)/shard_map/all_gather | solution.py:77
  20.7 7.5 %all-reduce.4 = (bf16[576]{0:T(1024)(128)(2,1)S(1)}, bf16[576]{0:T(1024)(128)(2,1)S(1)}) all-reduce(bf16[576]{0:T(1024)(128)(2,1)S(1)} %dynamic-update-slice, bf16[576]{0:T(1024)(128)(2,1)S(1)} %dynamic-update-slice.1), channel_id=1, replica_groups=mesh['dp'=4,'ctx'=2,'fsdp'=4] {'fsdp'}, use_global_device_ids=true, to_apply=%add | all-reduce | flops 1152 | bytes 4608
  29.7 10.2 %all_gather.35 = bf16[2,1024,192]{1,2,0:T(8,128)(2,1)} all-gather(bf16[2,512,192]{1,2,0:T(8,128)(2,1)S(1)} %convolution_convert_fusion.1), channel_id=1, replica_groups=mesh['dp'=4,'ctx'=2,'fsdp'=4] {'ctx'}, dimensions={1}, use_global_device_ids=true | all-gather | bytes 1179648 | tf_op jit(solution)/shard_map/all_gather | solution.py:130
  47.7 12.1 %all_gather.37 = bf16[2,1024,192]{1,2,0:T(8,128)(2,1)} all-gather(bf16[2,512,192]{1,2,0:T(8,128)(2,1)S(1)} %bitcast.265), channel_id=1, replica_groups=mesh['dp'=4,'ctx'=2,'fsdp'=4] {'ctx'}, dimensions={1}, use_global_device_ids=true | all-gather | bytes 1179648 | tf_op jit(solution)/shard_map/all_gather | solution.py:124
  59.9 8.6 %all_gather.38 = bf16[576,576]{1,0:T(8,128)(2,1)S(1)} all-gather(bf16[144,576]{1,0:T(8,128)(2,1)S(1)} %copy-done.35), channel_id=1, replica_groups=mesh['dp'=4,'ctx'=2,'fsdp'=4] {'fsdp'}, dimensions={0}, use_global_device_ids=true | all-gather | bytes 829440 | tf_op jit(solution)/shard_map/all_gather | solution.py:75
  74.0 19.5 %while.46 = (s32[]{:T(128)}, f32[2,3,3,512]{3,2,1,0:T(4,128)S(1)}, f32[2,3,3,512]{3,2,1,0:T(4,128)S(1)}, s32[]{:T(128)}, bf16[2,1024,3,64]{1,3,2,0:T(8,128)(2,1)...) while((s32[]{:T(128)}, f32[2,3,3,512]{3,2,1,0:T(4,128)S(1)}, ...), condition=%wide.region_4.5_spmd.clone, body=%wide.region_1.4_spmd.clone.sunk | while | flops 637291520 | bytes 40595632 | solution.py:163
  74.3 9.0 %fusion.174 = (f32[2,3,3,512]{3,2,1,0:T(4,128)S(1)}, f32[2,3,512,512,3]{3,2,4,1,0:T(8,128)}) fusion(pred[512,512]{0,1:T(8,128)(4,1)S(1)} %broadcast_compare_fusion.7, bf16[2,512,3,3,64]{1,4,3,2,0:T(8,128)(2,1)S(1)} %get-tuple-element.832, bf16[2,1024,3,64]{1,3,2,0:T(8,128)(2,1)} %get-tuple-element.831, s32[]{:T(128)S(6)} %select_n.110), kind=kOutput, calls=%fused_computation.34.clone.1 | convolution fusion | flops 618126336 | bytes 20746244 | tf_op jit(solution)/shard_map/while/body/gqhrd,gkhd->ghrqk/dot_general | solution.py:63
  83.3 10.2 %exponential_reduce_fusion.2 = f32[2,3,3,512]{3,2,1,0:T(4,128)S(1)} fusion(f32[2,3,512,512,3]{3,2,4,1,0:T(8,128)} %get-tuple-element.771, f32[2,3,3,512]{3,2,1,0:T(4,128)S(1)} %max.5, pred[512,512]{0,1:T(8,128)(4,1)S(1)} %broadcast_compare_fusion.7), kind=kLoop, calls=%fused_computation.33.clone.1 | loop fusion | flops 18865152 | bytes 19210240 | tf_op jit(solution)/shard_map/while/body/reduce_sum | solution.py:157
  95.9 12.6 %while.47 = (s32[]{:T(128)}, f32[2,512,3,3,64]{1,4,3,2,0:T(8,128)}, s32[]{:T(128)}, bf16[2,1024,3,64]{1,3,2,0:T(8,128)(2,1)}, bf16[2,1024,3,64]{1,3,2,0:T(8,128)...) while((s32[]{:T(128)}, f32[2,512,3,3,64]{1,4,3,2,0:T(8,128)}, ...), condition=%wide.region_6.7_spmd.clone, body=%wide.region_5.6_spmd.clone.sunk | while | flops 1227686912 | bytes 10805435 | solution.py:179
  98.1 10.4 %bitcast_add_fusion.4 = f32[2,512,3,3,64]{1,4,3,2,0:T(8,128)} fusion(f32[2,512,3,3,64]{1,4,3,2,0:T(8,128)} %get-tuple-element.851, f32[2,3,3,512]{3,2,1,0:T(4,128)} %get-tuple-element.868, pred[512,512]{1,0:T(8,128)(4,1)S(1)} %broadcast_compare_fusion.8, bf16[2,512,3,3,64]{4,3,2,1,0:T(4,128)(2,1)} %get-tuple-element.867, ...), kind=kOutput, calls=%fused_computation.50.clone.1 | convolution fusion | flops 1227423744 | bytes 8962052 | tf_op jit(solution)/shard_map/while/body/ghrqk,gkhd->gqhrd/dot_general | solution.py:175
  113.6 8.4 %all_gather.39 = bf16[576,576]{1,0:T(8,128)(2,1)S(1)} all-gather(bf16[144,576]{1,0:T(8,128)(2,1)S(1)} %copy-done.36), channel_id=1, replica_groups=mesh['dp'=4,'ctx'=2,'fsdp'=4] {'fsdp'}, dimensions={0}, use_global_device_ids=true | all-gather | bytes 829440 | tf_op jit(solution)/shard_map/all_gather | solution.py:78
  133.1 7.2 %fusion.104 = f32[2,512,1536]{2,1,0:T(8,128)} fusion(bf16[2,512,576]{1,2,0:T(8,128)(2,1)} %multiply_convert_fusion.3, bf16[576,1536]{1,0:T(8,128)(2,1)} %all-gather.6.cloned.1.call-done), kind=kOutput, calls=%fused_computation.122 | convolution fusion | flops 1811939328 | bytes 9240576 | tf_op jit(solution)/shard_map/gsd,df->gsf/dot_general | solution.py:196
  140.3 11.2 %multiply_convert_fusion.1 = (bf16[2,512,1536]{2,1,0:T(8,128)(2,1)S(1)}, bf16[2,512,1536]{2,1,0:T(8,128)(2,1)S(1)}, bf16[2,512,1536]{2,1,0:T(8,128)(2,1)}) fusion(f32[2,512,1536]{2,1,0:T(8,128)} %fusion.98, f32[2,512,1536]{2,1,0:T(8,128)} %fusion.104, bf16[2,512,576]{1,2,0:T(8,128)(2,1)} %multiply_convert_fusion.3, ...), kind=kOutput, calls=%fused_computation.87 | convolution fusion | flops 1835532288 | bytes 24969216 | tf_op jit(solution)/shard_map/gsd,df->gsf/dot_general | solution.py:195
  169.7 39.5 %while.49 = (s32[]{:T(128)}, bf16[2,512,2,384]{1,3,2,0:T(8,128)(2,1)}, s32[2]{0:T(128)S(1)}, s32[]{:T(128)}, bf16[2,1024,3,64]{1,3,2,0:T(8,128)(2,1)}, /*index=5...) while((s32[]{:T(128)}, ...), condition=%wide.region_15.16_spmd.clone, body=%wide.region_12.15_spmd.clone.sunk | while | flops 2465334272 | bytes 72477040 | solution.py:305
  171.1 34.8 %conditional.3 = (bf16[1,512,2,384]{1,3,2,0:T(8,128)(2,1)S(1)}) conditional(s32[]{:T(128)} %convert_element_type.194, () %tuple.125, (s32[]{:T(128)}, s32[512]{0:T(512)S(1)}, s32[]{:T(128)}, bf16[2,1024,3,64]{1,3,2,0:T(8,128)(2,1)}, bf16[2,512,3,3,64]{1,4,3,2,0:T(8,128)(2,1)S(1)}, /*index=5*/f32[2,3,3,512]{3,2,1,0:T(4,128)}, ...), branch_computations={%region_13.13_spmd, %region_14.14_spmd} | conditional | flops 2465334272 | bytes 70901880 | solution.py:303
  171.2 9.1 %fusion.29 = f32[2,3,512,512,3]{3,2,4,1,0:T(8,128)} fusion(bf16[2,512,3,3,64]{1,4,3,2,0:T(8,128)(2,1)S(1)} %get-tuple-element.285, bf16[2,1024,3,64]{1,3,2,0:T(8,128)(2,1)} %get-tuple-element.284, s32[]{:T(128)S(6)} %select_n.47), kind=kOutput, calls=%fused_computation.22 | convolution fusion | flops 603979776 | bytes 20447236 | tf_op jit(solution)/shard_map/while/body/eval_jaxpr/cond/branch_1_fun/gqhrd,gkhd->ghrqk/dot_general | solution.py:63
  180.5 12.0 %fusion.13 = bf16[2,3,512,64,1]{2,3,4,1,0:T(8,128)(2,1)} fusion(bf16[2,512,3,3,64]{1,4,3,2,0:T(8,128)(2,1)} %get-tuple-element.288, f32[2,3,512,512,3]{3,2,4,1,0:T(8,128)} %fusion.29, f32[2,3,3,512]{3,2,1,0:T(4,128)} %get-tuple-element.286, pred[512,512]{0,1:T(8,128)(4,1)S(1)} %broadcast_compare_fusion), kind=kOutput, calls=%fused_computation.11 | convolution fusion | flops 622854144 | bytes 20746240 | tf_op jit(solution)/shard_map/while/body/eval_jaxpr/cond/branch_1_fun/ghrqk,gqhrd->kghd/dot_general | solution.py:286
  193.8 12.0 %fusion.24 = bf16[2,3,512,64]{2,3,1,0:T(8,128)(2,1)S(1)} fusion(bf16[2,512,3,3,64]{1,4,3,2,0:T(8,128)(2,1)S(1)} %get-tuple-element.285, f32[2,3,512,512,3]{3,2,4,1,0:T(8,128)} %fusion.29, f32[2,3,3,512]{3,2,1,0:T(4,128)} %get-tuple-element.289, f32[2,3,3,512]{3,2,1,0:T(4,128)} %get-tuple-element.286, pred[512,512]{0,1:T(8,128)(4,1)S(1)} %broadcast_compare_fusion, ...), kind=kOutput, calls=%fused_computation.18 | convolution fusion | flops 1236664320 | bytes 22355968 | tf_op jit(solution)/shard_map/while/body/eval_jaxpr/cond/branch_1_fun/ghrqk,gqhrd->kghd/dot_general | solution.py:278
  214.8 25.2 %while.48 = (s32[]{:T(128)}, f32[2,512,3,3,64]{1,4,3,2,0:T(8,128)}, s32[]{:T(128)}, bf16[2,1024,3,64]{1,3,2,0:T(8,128)(2,1)}, bf16[2,512,3,3,64]{4,3,2,1,0:T(4,1...) while((s32[]{:T(128)}, f32[2,512,3,3,64]{1,4,3,2,0:T(8,128)}, ...), condition=%wide.region_11.12_spmd.clone, body=%wide.region_10.11_spmd.clone.sunk | while | flops 1841103872 | bytes 47400136 | solution.py:247
  216.4 7.8 %fusion.185 = f32[2,3,512,512,3]{2,3,4,1,0:T(8,128)} fusion(bf16[2,512,3,3,64]{4,3,2,1,0:T(4,128)(2,1)S(1)} %get-tuple-element.948, bf16[2,512,3,64,1]{3,2,1,0,4:T(4,128)(2,1)S(1)} %dynamic-slice_bitcast_fusion.3), kind=kOutput, calls=%fused_computation.72.clone.1 | convolution fusion | flops 603979776 | bytes 20447232 | tf_op jit(solution)/shard_map/while/body/gqhrd,gkhd->ghrqk/dot_general | solution.py:238
  224.4 15.4 %bitcast_add_fusion.5 = f32[2,512,3,3,64]{1,4,3,2,0:T(8,128)} fusion(f32[2,512,3,3,64]{1,4,3,2,0:T(8,128)} %get-tuple-element.928, f32[2,3,512,512,3]{2,3,4,1,0:T(8,128)} %fusion.185, f32[2,3,3,512]{3,2,1,0:T(4,128)S(1)} %get-tuple-element.949, f32[2,3,3,512]{3,2,1,0:T(4,128)} %get-tuple-element.946, ...), kind=kOutput, calls=%fused_computation.71.clone.1 | convolution fusion | flops 1236860928 | bytes 25895936 | tf_op jit(solution)/shard_map/while/body/ghrqk,gkhd->gqhrd/dot_general | solution.py:242
  259.9 46.3 %reduce-scatter.2.cloned.1.call-done = bf16[512,2,384]{0,2,1:T(8,128)(2,1)} async-done(((bf16[1024,2,384]{0,2,1:T(8,128)(2,1)}), bf16[512,2,384]{0,2,1:T(8,128)(2,1)}) %reduce-scatter.2.cloned.1.call-update) | async-done | bytes 786448 | tf_op jit(solution)/shard_map/reduce_scatter | solution.py:307
  324.0 88.5 %all-reduce.2 = (f32[576]{0:T(1024)}, f32[576]{0:T(1024)}) all-reduce(f32[576]{0:T(1024)} %get-tuple-element.444, f32[576]{0:T(1024)} %get-tuple-element.442), channel_id=1, replica_groups=mesh['dp'=4,'ctx'=2,'fsdp'=4] {'dp','ctx','fsdp'}, use_global_device_ids=true, to_apply=%region_19.20 | all-reduce | flops 1152 | bytes 9216 | tf_op jit(solution)/shard_map/psum | solution.py:361
  418.9 204.6 %all-reduce.7.cloned.1.call-done = (f32[576,576]{1,0:T(8,128)}, f32[576,192]{1,0:T(8,128)}, f32[576,192]{1,0:T(8,128)}, f32[576,576]{1,0:T(8,128)}, f32[576,1536...) async-done(((f32[576,576]{1,0:T(8,128)}, f32[576,192]{1,0:T(8,128)}, f32[576,192]{1,0:T(8,128)}, f32[576,576]{1,0:T(8,128)}, f32[576,1536]{1,0:T(8,128)}, ...) | async-done | bytes 14155792 | tf_op jit(solution)/shard_map/psum | solution.py:361
  (209 shorter events, 123.5 us)
Async XLA Ops:
  7.2 21.1 %copy-start.5 = (bf16[2,512,576]{1,2,0:T(8,128)(2,1)S(1)}, bf16[2,512,576]{1,2,0:T(8,128)(2,1)}, u32[]{:S(2)}) copy-start(bf16[2,512,576]{1,2,0:T(8,128)(2,1)} %param.21) | copy-start | bytes 3538948
  7.2 118.7 %all-gather.8.cloned.1.call-start = ((), (), s32[]{:S(2)}) async-start(), calls=%async_computation.3 | async-start | bytes 2211840 | tf_op jit(solution)/shard_map/all_gather | solution.py:82
  7.9 125.2 %all-gather.6.cloned.1.call-start = ((), (), s32[]{:S(2)}) async-start(), calls=%async_computation.2 | async-start | bytes 2211840 | tf_op jit(solution)/shard_map/all_gather | solution.py:81
  8.7 131.6 %all-gather.4.cloned.1.call-start = ((), (), s32[]{:S(2)}) async-start(), calls=%async_computation.1 | async-start | bytes 2211840 | tf_op jit(solution)/shard_map/all_gather | solution.py:80
  9.4 296.8 %reduce-scatter.2.cloned.1.call-start = ((), (), s32[]{:S(2)}) async-start(), calls=%async_computation.4 | async-start | bytes 2359296 | tf_op jit(solution)/shard_map/reduce_scatter | solution.py:307
  17.1 22.8 %copy-start.23 = (bf16[576,192]{1,0:T(8,128)(2,1)}, bf16[576,192]{1,0:T(8,128)(2,1)S(1)}, u32[]{:S(2)}) copy-start(bf16[576,192]{1,0:T(8,128)(2,1)S(1)} %all_gather.34) | copy-start | bytes 663556
  28.3 40.3 %copy-start.41 = (f32[576]{0:T(1024)}, f32[576]{0:T(1024)S(1)}, u32[]{:S(2)}) copy-start(f32[576]{0:T(1024)S(1)} %convert_element_type.100) | copy-start | bytes 6916
  28.5 11.4 %copy-start.37 = (bf16[144,192]{1,0:T(8,128)(2,1)S(1)}, bf16[144,192]{1,0:T(8,128)(2,1)}, u32[]{:S(2)}) copy-start(bf16[144,192]{1,0:T(8,128)(2,1)} %param.24) | copy-start | bytes 165892
  29.1 39.4 %copy-start.39 = (f32[2,512]{1,0:T(2,128)}, f32[2,512]{1,0:T(2,128)S(1)}, u32[]{:S(2)}) copy-start(f32[2,512]{1,0:T(2,128)S(1)} %get-tuple-element.551) | copy-start | bytes 12292
  47.2 12.7 %copy-start.35 = (bf16[144,576]{1,0:T(8,128)(2,1)S(1)}, bf16[144,576]{1,0:T(8,128)(2,1)}, u32[]{:S(2)}) copy-start(bf16[144,576]{1,0:T(8,128)(2,1)} %param.23) | copy-start | bytes 497668
  47.5 22.2 %copy-start.15 = (f32[512,32]{0,1:T(8,128)}, f32[512,32]{0,1:T(8,128)S(1)}, u32[]{:S(2)}) copy-start(f32[512,32]{0,1:T(8,128)S(1)} %get-tuple-element.554) | copy-start | bytes 196612
  47.6 22.2 %copy-start.18 = (f32[512,32]{0,1:T(8,128)}, f32[512,32]{0,1:T(8,128)S(1)}, u32[]{:S(2)}) copy-start(f32[512,32]{0,1:T(8,128)S(1)} %get-tuple-element.555) | copy-start | bytes 196612
  108.5 4.2 copy-start.2
  112.7 9.4 %copy-start.6 = (bf16[2,512,576]{1,2,0:T(8,128)(2,1)S(1)}, bf16[2,512,576]{1,2,0:T(8,128)(2,1)}, u32[]{:S(2)}) copy-start(bf16[2,512,576]{1,2,0:T(8,128)(2,1)} %param.21) | copy-start | bytes 3538948
  112.8 10.4 %copy-start.12 = (bf16[2,512,3,3,64]{1,4,3,2,0:T(8,128)(2,1)}, bf16[2,512,3,3,64]{1,4,3,2,0:T(8,128)(2,1)S(1)}, u32[]{:S(2)}) copy-start(bf16[2,512,3,3,64]{1,4,3,2,0:T(8,128)(2,1)S(1)} %convert_element_type.105) | copy-start | bytes 3538948
  140.3 11.2 %copy-start.45 = (bf16[576,1536]{1,0:T(8,128)(2,1)S(1)}, bf16[576,1536]{1,0:T(8,128)(2,1)}, u32[]{:S(2)}) copy-start(bf16[576,1536]{1,0:T(8,128)(2,1)} %all-gather.6.cloned.1.call-done) | copy-start | bytes 5308420
  151.5 4.4 copy-start.46
  180.5 12.0 %copy-start.1 = (bf16[2,1024,3,64]{3,2,1,0:T(4,128)(2,1)S(1)}, bf16[2,1024,3,64]{3,2,1,0:T(4,128)(2,1)}, u32[]{:S(2)}) copy-start(bf16[2,1024,3,64]{3,2,1,0:T(4,128)(2,1)} %get-tuple-element.287) | copy-start | bytes 2359300 | tf_op jit(solution)/shard_map/while/body/eval_jaxpr/cond
  193.8 12.0 %copy-start.8 = (bf16[2,3,512,64,1]{2,3,4,1,0:T(8,128)(2,1)S(1)}, bf16[2,3,512,64,1]{2,3,4,1,0:T(8,128)(2,1)}, u32[]{:S(2)}) copy-start(bf16[2,3,512,64,1]{2,3,4,1,0:T(8,128)(2,1)} %fusion.13) | copy-start | bytes 1179652 | tf_op jit(solution)/shard_map/while/body/eval_jaxpr/cond
  212.1 411.5 %all-reduce.7.cloned.1.call-start = ((), (), s32[]{:S(2)}) async-start(), calls=%async_computation.5 | async-start | bytes 29491200 | tf_op jit(solution)/shard_map/psum | solution.py:361
  248.5 3.9 copy-start.51
  314.8 5.0 copy-start.22
  314.8 5.0 copy-start.26
  321.1 94.1 %copy-start.43 = (f32[2,512]{1,0:T(2,128)S(1)}, f32[2,512]{1,0:T(2,128)}, u32[]{:S(2)}) copy-start(f32[2,512]{1,0:T(2,128)} %get-tuple-element.550) | copy-start | bytes 12292
  (33 other events, 67.8 us)
Sparse Core Ops, SparseCore 0:
  9.6 23.5 all-gather.7
  34.7 21.1 all-gather.5
  57.5 21.1 all-gather.3
  212.2 93.9 reduce-scatter.1
  314.2 309.3 all-reduce.6
where the time goes:
time: 649 us; the launch traced here: 639 us
  waiting for transfers between devices  253 us (39%)
  blocking collectives  150 us (23%)
  matrix products  142 us (22%)
  local copies, waits for them, and re-layouts  53.7 us (8%)
  other arithmetic  23.2 us (4%)
  between operations  15.4 us (2%)
    psum x1, waiting for transfers between devices, local(): lax.psum((grad_gain1, grad_query, grad_key, grad_value, grad_out, grad_ga...  205 us
    psum x1, blocking collectives, local(): lax.psum((grad_gain1, grad_query, grad_key, grad_value, grad_out, grad_ga...  88.5 us
    reduce_scatter x1, waiting for transfers between devices, local(): lax.psum_scatter(terms.reshape(row_total, query_group_count, 2 * key_valu...  46.3 us
    unnamed x108, local copies, waits for them, and re-layouts  27.2 us
    dot_general x2, matrix products, block_scores(): jnp.einsum('gqhrd,gkhd->ghrqk', query_block, key_block, preferred_element...  18.1 us
    dot_general x1, matrix products, query_grad_step(): jnp.einsum('ghrqk,gkhd->gqhrd', score_grad, key_block, preferred_element_...  15.4 us
  transfers between devices with their start and end apart: 5, of which 2 were waited for; matrix products, arithmetic and copies ran while one was open for 20% of the time, Pallas kernels for 0%

commit v1 on v0

--- a/solution.py
+++ b/solution.py
@@ -1,8 +1,11 @@
+import functools
 import math
 
 import jax
 import jax.numpy as jnp
 from jax import lax
+from jax.experimental import pallas as pl
+from jax.experimental.pallas import tpu as pltpu
 from jax.sharding import PartitionSpec as P
 
 QUERY_HEADS = 9
@@ -67,7 +70,7 @@
     return jnp.where(visible, scores, MASKED)
 
 
-def local(
+def split_context(
     tokens, norm1_gain, w_query, w_key, w_value, w_out, norm2_gain, w_gate, w_up, w_down, out_grad
 ):
     gain1, wq_full, wk_full, wv_full, wo_full, gain2, wg_full, wu_full, wd_full = (
@@ -395,9 +398,620 @@
     )
 
 
+WIDTH = 576
+QUERY_WIDTH = QUERY_HEADS * HEAD_SIZE
+KEY_WIDTH = KEY_VALUE_HEADS * HEAD_SIZE
+ROTATED = QUERY_HEADS + KEY_VALUE_HEADS
+REPEAT = QUERY_HEADS // KEY_VALUE_HEADS
+HALF = HEAD_SIZE // 2
+PACKED = QUERY_WIDTH + 2 * KEY_WIDTH + 64
+GAIN_AT = QUERY_WIDTH + 2 * KEY_WIDTH - (PACKED - 128)
+TILE = 256
+VMEM_LIMIT = 52 * 1024 * 1024
+F32 = jnp.float32
+BF16 = jnp.bfloat16
+
+
+def mm(a, b):
+    return jnp.dot(a, b, preferred_element_type=F32)
+
+
+def mm_nt(a, b):
+    return lax.dot_general(a, b, (((1,), (1,)), ((), ())), preferred_element_type=F32)
+
+
+def flip(tensor):
+    return tensor.astype(F32).T
+
+
+def rows_at(index, size):
+    return pl.ds(pl.multiple_of(index * size, size), size)
+
+
+def attend_kernel(
+    place,
+    mine,
+    theirs,
+    w_own,
+    w_y,
+    w_core,
+    w_both,
+    cosine,
+    sine,
+    x_seq,
+    normed,
+    packed,
+    gains,
+    qkv_t,
+    log_total,
+    attended_t,
+    key_rows,
+):
+    me, shard = place[0], place[1]
+    half_rows = mine.shape[0]
+    sequence = 2 * half_rows
+    x_seq[rows_at(me, half_rows), :] = mine[...]
+    x_seq[rows_at(1 - me, half_rows), :] = theirs[...]
+    rows = w_own.shape[0]
+    for bits, piece in ((0, w_own), (2, w_y), (1, w_core), (3, w_both)):
+        packed[rows_at(shard ^ bits, rows), :] = piece[...]
+    gain_rows = flip(packed[:, PACKED - 128 :])
+    gains[...] = gain_rows[GAIN_AT : GAIN_AT + 8, :]
+    gain1 = gain_rows[GAIN_AT : GAIN_AT + 1, :]
+
+    def project(tile, carry):
+        at = rows_at(tile, TILE)
+        x = x_seq[at, :].astype(F32)
+        scale = lax.rsqrt(jnp.mean(x * x, axis=-1, keepdims=True) + EPSILON)
+        normed_tile = (x * scale * gain1).astype(BF16)
+        normed[at, :] = normed_tile
+        turned = mm(normed_tile, packed[...]).T
+        cos, sin = cosine[:, at], sine[:, at]
+        for head in range(ROTATED):
+            a = turned[head * HEAD_SIZE : head * HEAD_SIZE + HALF, :]
+            b = turned[head * HEAD_SIZE + HALF : (head + 1) * HEAD_SIZE, :]
+            both = jnp.concatenate([a * cos - b * sin, b * cos + a * sin], 0)
+            if head < QUERY_HEADS:
+                both = both * 0.125
+            else:
+                key_rows[head - QUERY_HEADS, at, :] = both.T.astype(BF16)
+            qkv_t[head * HEAD_SIZE : (head + 1) * HEAD_SIZE, at] = both.astype(BF16)
+        values = turned[ROTATED * HEAD_SIZE : ROTATED * HEAD_SIZE + KEY_WIDTH, :]
+        qkv_t[ROTATED * HEAD_SIZE :, at] = values.astype(BF16)
+        return carry
+
+    lax.fori_loop(0, sequence // TILE, project, 0)
+
+    def one_head(head, carry):
+        group = head // REPEAT
+        head_rows = rows_at(head, HEAD_SIZE)
+        value_rows = rows_at(ROTATED + group, HEAD_SIZE)
+        for tile in range(sequence // TILE):
+            extent = (tile + 1) * TILE
+            cols = slice(tile * TILE, extent)
+            queries = qkv_t[head_rows, cols]
+            scores = mm(key_rows[group, :extent, :], queries)
+            visible = lax.broadcasted_iota(jnp.int32, (TILE, TILE), 0) <= lax.broadcasted_iota(
+                jnp.int32, (TILE, TILE), 1
+            )
+            last = jnp.where(visible, scores[tile * TILE :, :], MASKED)
+            scores = last if tile == 0 else jnp.concatenate([scores[: tile * TILE, :], last], 0)
+            top = jnp.max(scores, axis=0, keepdims=True)
+            weights = jnp.exp(scores - top)
+            total = jnp.sum(weights, axis=0, keepdims=True)
+            mixed = mm(qkv_t[value_rows, :extent], weights.astype(BF16))
+            attended_t[head_rows, cols] = (mixed * (1.0 / total)).astype(BF16)
+            log_total[group, pl.ds(head - group * REPEAT, 1), cols] = top + jnp.log(total)
+        return carry
+
+    lax.fori_loop(0, QUERY_HEADS, one_head, 0)
+
+
+def feed_forward_kernel(
+    place,
+    x_seq,
+    attended_t,
+    dy_mine,
+    dy_theirs,
+    gains,
+    a_own,
+    a_y,
+    a_core,
+    a_both,
+    b_own,
+    b_y,
+    b_core,
+    b_both,
+    out_keep,
+    out_send,
+    middle_grad_out,
+    attended_grad_t,
+    keep_b,
+    send_b,
+    keep_a,
+    send_a,
+    gain_grad,
+    w_out,
+    w_down,
+    w_gate,
+    w_up,
+    dy_seq,
+    out_seq,
+    normed_t,
+    hidden,
+    gate_grad,
+    up_grad,
+    branch_grad,
+    total,
+    total_tall,
+):
+    me, shard = place[0], place[1]
+    half_rows = dy_mine.shape[0]
+    sequence = 2 * half_rows
+    dy_seq[rows_at(me, half_rows), :] = dy_mine[...]
+    dy_seq[rows_at(1 - me, half_rows), :] = dy_theirs[...]
+    rows = b_own.shape[0] // 2
+    down_rows = a_own.shape[0] - rows
+    for bits, a, b in ((0, a_own, b_own), (2, a_y, b_y), (1, a_core, b_core), (3, a_both, b_both)):
+        w_out[rows_at(shard ^ bits, rows), :] = a[:rows, :]
+        w_down[rows_at(shard ^ bits, down_rows), :] = a[rows:, :]
+        w_gate[rows_at(shard ^ bits, rows), :] = b[:rows, :]
+        w_up[rows_at(shard ^ bits, rows), :] = b[rows:, :]
+    gain2 = gains[1:2, :]
+    gain_grad[...] = jnp.zeros_like(gain_grad)
+
+    def one_tile(tile, carry):
+        at = rows_at(tile, TILE)
+        attended = flip(attended_t[:, at]).astype(BF16)
+        middle = x_seq[at, :].astype(F32) + mm(attended, w_out[...])
+        scale = lax.rsqrt(jnp.mean(middle * middle, axis=-1, keepdims=True) + EPSILON)
+        ready = middle * scale
+        normed = ready * gain2
+        normed_t[:, at] = normed.T.astype(BF16)
+        normed = normed.astype(BF16)
+        gate = mm(normed, w_gate[...])
+        up = mm(normed, w_up[...])
+        sig = 1.0 / (1.0 + jnp.exp(-gate))
+        silu = gate * sig
+        hidden_tile = (silu * up).astype(BF16)
+        hidden[at, :] = hidden_tile
+        out_seq[at, :] = (middle + mm(hidden_tile, w_down[...])).astype(BF16)
+        dy = dy_seq[at, :]
+        hidden_grad = mm_nt(dy, w_down[...])
+        gate_tile = (hidden_grad * up * sig * (1.0 + gate * (1.0 - sig))).astype(BF16)
+        up_tile = (hidden_grad * silu).astype(BF16)
+        gate_grad[at, :] = gate_tile
+        up_grad[at, :] = up_tile
+        normed_grad = mm_nt(gate_tile, w_gate[...]) + mm_nt(up_tile, w_up[...])
+        gain_grad[0:1, :] += jnp.sum(normed_grad * ready, axis=0, keepdims=True)
+        scaled = normed_grad * gain2
+        middle_grad = (
+            dy.astype(F32)
+            + scale * scaled
+            - middle * (scale * scale * scale) * jnp.mean(scaled * middle, axis=-1, keepdims=True)
+        )
+        middle_grad_out[at, :] = middle_grad
+        branch = middle_grad.astype(BF16)
+        branch_grad[at, :] = branch
+        attended_grad_t[:, at] = mm_nt(branch, w_out[...]).T.astype(BF16)
+        return carry
+
+    lax.fori_loop(0, sequence // TILE, one_tile, 0)
+    out_keep[...] = out_seq[rows_at(me, half_rows), :]
+    out_send[...] = out_seq[rows_at(1 - me, half_rows), :]
+    wide = gate_grad.shape[1]
+    for part, grads in ((0, gate_grad), (1, up_grad)):
+        for first in range(0, wide, 512):
+            cols = slice(first, min(first + 512, wide))
+            total[:, cols] = mm(normed_t[...], grads[:, cols]).astype(BF16)
+        at = slice(part * rows, (part + 1) * rows)
+        for y_bit in range(2):
+            keep_b[y_bit, at, :] = total[rows_at(shard ^ (2 * y_bit), rows), :]
+            send_b[y_bit, at, :] = total[rows_at(shard ^ (2 * y_bit + 1), rows), :]
+    for first in range(0, wide, 512):
+        cols = slice(first, min(first + 512, wide))
+        total_tall[cols, :] = mm(flip(hidden[:, cols]).astype(BF16), dy_seq[...]).astype(BF16)
+    for y_bit in range(2):
+        keep_a[y_bit, rows:, :] = total_tall[rows_at(shard ^ (2 * y_bit), down_rows), :]
+        send_a[y_bit, rows:, :] = total_tall[rows_at(shard ^ (2 * y_bit + 1), down_rows), :]
+    total[:, :QUERY_WIDTH] = mm(attended_t[...], branch_grad[...]).astype(BF16)
+    for y_bit in range(2):
+        keep_a[y_bit, :rows, :] = total[rows_at(shard ^ (2 * y_bit), rows), :QUERY_WIDTH]
+        send_a[y_bit, :rows, :] = total[rows_at(shard ^ (2 * y_bit + 1), rows), :QUERY_WIDTH]
+
+
+def attend_back_kernel(
+    queries_t,
+    keys_t,
+    values_t,
+    log_total,
+    attended_t,
+    grad_t,
+    cosine,
+    sine,
+    dq_out,
+    dk_out,
+    dv_out,
+    keys,
+    values,
+    dk,
+    dv,
+    dq,
+):
+    sequence = keys_t.shape[1]
+    keys[...] = flip(keys_t[...]).astype(BF16)
+    values[...] = flip(values_t[...]).astype(BF16)
+    dk[...] = jnp.zeros_like(dk)
+    dv[...] = jnp.zeros_like(dv)
+
+    def back(a, b, cos, sin):
+        return (a * cos + b * sin).astype(BF16), (b * cos - a * sin).astype(BF16)
+
+    def one_head(head, carry):
+        head_rows = rows_at(head, HEAD_SIZE)
+        for tile in range(sequence // TILE):
+            extent = (tile + 1) * TILE
+            cols = slice(tile * TILE, extent)
+            q_t = queries_t[head_rows, cols]
+            do_t = grad_t[head_rows, cols]
+            do_wide = do_t.astype(F32)
+            delta = jnp.sum(
+                do_wide * attended_t[head_rows, cols].astype(F32), axis=0, keepdims=True
+            )
+            scores = mm(keys[:extent, :], q_t)
+            visible = lax.broadcasted_iota(jnp.int32, (TILE, TILE), 0) <= lax.broadcasted_iota(
+                jnp.int32, (TILE, TILE), 1
+            )
+            last = jnp.where(visible, scores[tile * TILE :, :], MASKED)
+            scores = last if tile == 0 else jnp.concatenate([scores[: tile * TILE, :], last], 0)
+            probs = jnp.exp(scores - log_total[0, pl.ds(head, 1), cols])
+            dprob = mm(values[:extent, :], do_t)
+            score_grad = (probs * (dprob - delta)).astype(BF16)
+            dv[:extent, :] += mm(probs.astype(BF16), do_wide.T.astype(BF16))
+            dk[:extent, :] += mm(score_grad, flip(q_t).astype(BF16))
+            dq[:, cols] = mm(keys_t[:, :extent], score_grad) * 0.125
+        cos, sin = cosine[...], sine[...]
+        a, b = back(dq[:HALF, :], dq[HALF:, :], cos, sin)
+        dq_out[pl.ds(pl.multiple_of(head * HEAD_SIZE, HEAD_SIZE), HALF), :] = a
+        dq_out[pl.ds(pl.multiple_of(head * HEAD_SIZE + HALF, HALF), HALF), :] = b
+        return carry
+
+    lax.fori_loop(0, queries_t.shape[0] // HEAD_SIZE, one_head, 0)
+    turned = dk[...].T
+    a, b = back(turned[:HALF, :], turned[HALF:, :], cosine[...], sine[...])
+    dk_out[:HALF, :] = a
+    dk_out[HALF:, :] = b
+    dv_out[...] = dv[...].T.astype(BF16)
+
+
+def input_kernel(
+    place,
+    x_seq,
+    normed,
+    packed,
+    gains,
+    gain2_grad,
+    middle_grad,
+    *rest,
+):
+    heads = rest[: 3 * KEY_VALUE_HEADS]
+    keep_w, send_w, keep_x, send_x, joined, grad_seq, total = rest[3 * KEY_VALUE_HEADS :]
+    me, shard = place[0], place[1]
+    half_rows = keep_x.shape[0]
+    sequence = 2 * half_rows
+    group_width = REPEAT * HEAD_SIZE
+    for group in range(KEY_VALUE_HEADS):
+        dq, dk, dv = heads[3 * group : 3 * group + 3]
+        joined[group * group_width : (group + 1) * group_width, :] = dq[...]
+        at = QUERY_WIDTH + group * HEAD_SIZE
+        joined[at : at + HEAD_SIZE, :] = dk[...]
+        at = QUERY_WIDTH + KEY_WIDTH + group * HEAD_SIZE
+        joined[at : at + HEAD_SIZE, :] = dv[...]
+    joined[QUERY_WIDTH + 2 * KEY_WIDTH :, :] = jnp.zeros(
+        (PACKED - QUERY_WIDTH - 2 * KEY_WIDTH, sequence), BF16
+    )
+    gain1 = gains[0:1, :]
+    gain1_grad = jnp.zeros((1, WIDTH), F32)
+    for tile in range(sequence // TILE):
+        at = slice(tile * TILE, (tile + 1) * TILE)
+        normed_grad = mm(packed[...], joined[:, at]).T
+        x = x_seq[at, :].astype(F32)
+        scale = lax.rsqrt(jnp.mean(x * x, axis=-1, keepdims=True) + EPSILON)
+        gain1_grad += jnp.sum(normed_grad * x * scale, axis=0, keepdims=True)
+        scaled = normed_grad * gain1
+        grad_seq[at, :] = (
+            middle_grad[at, :]
+            + scale * scaled
+            - x * (scale * scale * scale) * jnp.mean(scaled * x, axis=-1, keepdims=True)
+        )
+    keep_x[...] = grad_seq[rows_at(me, half_rows), :]
+    send_x[...] = grad_seq[rows_at(1 - me, half_rows), :].astype(BF16)
+    for first in range(0, PACKED, TILE):
+        at = slice(first, first + TILE)
+        total[:, at] = mm(joined[at, :], normed[...]).T.astype(BF16)
+    row = lax.broadcasted_iota(jnp.int32, (128, WIDTH), 0)
+    gain_rows = jnp.where(row == GAIN_AT, gain1_grad, 0.0) + jnp.where(
+        row == GAIN_AT + 1, gain2_grad[0:1, :], 0.0
+    )
+    lane = lax.broadcasted_iota(jnp.int32, (WIDTH, 128), 1)
+    last = total[:, PACKED - 128 :].astype(F32)
+    total[:, PACKED - 128 :] = jnp.where(lane < GAIN_AT, last, gain_rows.T).astype(BF16)
+    rows = keep_w.shape[1]
+    for y_bit in range(2):
+        keep_w[y_bit] = total[rows_at(shard ^ (2 * y_bit), rows), :]
+        send_w[y_bit] = total[rows_at(shard ^ (2 * y_bit + 1), rows), :]
+
+
+def call(kernel, out, scratch, flops, exps, args, name):
+    shapes = [jax.ShapeDtypeStruct(s, d) for s, d in out]
+    moved = sum(a.size * a.dtype.itemsize for a in args[1:]) + sum(
+        s.size * s.dtype.itemsize for s in shapes
+    )
+    in_specs = [pl.BlockSpec(memory_space=pltpu.SMEM)] + [
+        pl.BlockSpec(memory_space=pltpu.VMEM)
+    ] * (len(args) - 1)
+    return pl.pallas_call(
+        kernel,
+        out_shape=shapes,
+        in_specs=in_specs,
+        out_specs=[pl.BlockSpec(memory_space=pltpu.VMEM)] * len(shapes),
+        scratch_shapes=[pltpu.VMEM(s, d) for s, d in scratch],
+        compiler_params=pltpu.CompilerParams(vmem_limit_bytes=VMEM_LIMIT),
+        cost_estimate=pl.CostEstimate(flops=flops, bytes_accessed=moved, transcendentals=exps),
+        name=name,
+    )(*args)
+
+
+def attend_back(group, qkv_t, log_total, attended_t, grad_t, cosine, sine):
+    sequence = qkv_t.shape[1]
+    group_width = REPEAT * HEAD_SIZE
+
+    def rows_of(size, index):
+        return pl.BlockSpec((size, sequence), lambda step: (index, 0))
+
+    flops = 5 * REPEAT * sequence * sequence * HEAD_SIZE * 2
+    return pl.pallas_call(
+        attend_back_kernel,
+        grid=(1,),
+        out_shape=[
+            jax.ShapeDtypeStruct((group_width, sequence), BF16),
+            jax.ShapeDtypeStruct((HEAD_SIZE, sequence), BF16),
+            jax.ShapeDtypeStruct((HEAD_SIZE, sequence), BF16),
+        ],
+        in_specs=[
+            rows_of(group_width, group),
+            rows_of(HEAD_SIZE, QUERY_HEADS + group),
+            rows_of(HEAD_SIZE, ROTATED + group),
+            pl.BlockSpec((1, 8, sequence), lambda step: (group, 0, 0)),
+            rows_of(group_width, group),
+            rows_of(group_width, group),
+            rows_of(HALF, 0),
+            rows_of(HALF, 0),
+        ],
+        out_specs=[rows_of(group_width, 0), rows_of(HEAD_SIZE, 0), rows_of(HEAD_SIZE, 0)],
+        scratch_shapes=[
+            pltpu.VMEM((sequence, HEAD_SIZE), BF16),
+            pltpu.VMEM((sequence, HEAD_SIZE), BF16),
+            pltpu.VMEM((sequence, HEAD_SIZE), F32),
+            pltpu.VMEM((sequence, HEAD_SIZE), F32),
+            pltpu.VMEM((HEAD_SIZE, sequence), F32),
+        ],
+        compiler_params=pltpu.CompilerParams(vmem_limit_bytes=VMEM_LIMIT),
+        cost_estimate=pl.CostEstimate(
+            flops=flops, bytes_accessed=4_000_000, transcendentals=REPEAT * sequence * sequence
+        ),
+        name="attend_back",
+    )(qkv_t, qkv_t, qkv_t, log_total, attended_t, grad_t, cosine, sine)
+
+
+def across(tensor, bit):
+    return lax.ppermute(tensor, "fsdp", [(i, i ^ bit) for i in range(4)])
+
+
+def over_context(tensor):
+    return lax.ppermute(tensor, "ctx", [(0, 1), (1, 0)])
+
+
+def after(tensor, *done):
+    return lax.optimization_barrier((tensor, *done))[0]
+
+
+def add(a, b):
+    return (a.astype(F32) + b.astype(F32)).astype(BF16)
+
+
+def sum_line(part):
+    size = lax.axis_size("dp")
+    at = lax.axis_index("dp")
+    middle = size // 2
+    for step in range(middle - 1):
+        pairs = [(step, step + 1), (size - 1 - step, size - 2 - step)]
+        part = add(part, lax.ppermute(part, "dp", pairs))
+    part = add(part, lax.ppermute(part, "dp", [(middle - 1, middle), (middle, middle - 1)]))
+    for step in range(middle - 2, -1, -1):
+        pairs = [(step + 1, step), (size - 2 - step, size - 1 - step)]
+        got = lax.ppermute(part, "dp", pairs)
+        part = jnp.where((at == step) | (at == size - 1 - step), got, part)
+    return part
+
+
+def reduce_shard(keep, send, axis):
+    me = lax.axis_index("ctx")
+    pair = add(keep, across(send, 1))
+    own = add(pair[0], across(pair[1], 2))
+    low, high = jnp.split(own, 2, axis)
+    part = add(jnp.where(me == 0, low, high), over_context(jnp.where(me == 0, high, low)))
+    part = sum_line(part)
+    other = over_context(part)
+    return (
+        jnp.where(me == 0, part, other).astype(F32),
+        jnp.where(me == 0, other, part).astype(F32),
+    )
+
+
+def gather_pieces(own, *done):
+    first = after(own, *done) if done else own
+    y_piece = across(first, 2)
+    return own, y_piece, across(first, 1), across(y_piece, 1)
+
+
+def whole_sequences(
+    tokens, norm1_gain, w_query, w_key, w_value, w_out, norm2_gain, w_gate, w_up, w_down, out_grad
+):
+    half_rows, width = tokens.shape[1:]
+    sequence = 2 * half_rows
+    rows = w_query.shape[0]
+    down_rows = w_down.shape[0]
+    hidden_width = w_gate.shape[1]
+    me = lax.axis_index("ctx")
+    place = jnp.stack([me, lax.axis_index("fsdp")]).astype(jnp.int32)
+
+    packed = jnp.concatenate(
+        [
+            w_query,
+            w_key,
+            w_value,
+            norm1_gain[:, None],
+            norm2_gain[:, None],
+            jnp.zeros((rows, PACKED - QUERY_WIDTH - 2 * KEY_WIDTH - 2), BF16),
+        ],
+        1,
+    )
+    packed_pieces = gather_pieces(packed)
+    tokens_mine = lax.dynamic_index_in_dim(tokens, me, 0, False)
+    tokens_theirs = over_context(lax.dynamic_index_in_dim(tokens, 1 - me, 0, False))
+    a_pieces = gather_pieces(jnp.concatenate([w_out, w_down], 0), packed_pieces[1])
+    b_pieces = gather_pieces(jnp.concatenate([w_gate, w_up], 0), packed_pieces[1])
+    dy_mine = lax.dynamic_index_in_dim(out_grad, me, 0, False)
+    dy_theirs = over_context(
+        after(lax.dynamic_index_in_dim(out_grad, 1 - me, 0, False), tokens_theirs)
+    )
+
+    cosine, sine = rope_tables(jnp.arange(sequence, dtype=jnp.int32), HEAD_SIZE)
+    cosine, sine = cosine.T, sine.T
+
+    pairs = sequence * sequence
+    x_seq, normed, packed_all, gains, qkv_t, log_total, attended_t = call(
+        attend_kernel,
+        [
+            ((sequence, width), BF16),
+            ((sequence, width), BF16),
+            ((width, PACKED), BF16),
+            ((8, width), F32),
+            ((QUERY_WIDTH + 2 * KEY_WIDTH, sequence), BF16),
+            ((KEY_VALUE_HEADS, 8, sequence), F32),
+            ((QUERY_WIDTH, sequence), BF16),
+        ],
+        [((KEY_VALUE_HEADS, sequence, HEAD_SIZE), BF16)],
+        2 * sequence * width * PACKED + 4 * QUERY_WIDTH * pairs,
+        QUERY_HEADS * pairs,
+        (place, tokens_mine, tokens_theirs, *packed_pieces, cosine, sine),
+        "attend",
+    )
+
+    (
+        out_keep,
+        out_send,
+        middle_grad,
+        grad_t,
+        keep_b,
+        send_b,
+        keep_a,
+        send_a,
+        gain2_grad,
+    ) = call(
+        feed_forward_kernel,
+        [
+            ((half_rows, width), BF16),
+            ((half_rows, width), BF16),
+            ((sequence, width), F32),
+            ((QUERY_WIDTH, sequence), BF16),
+            ((2, 2 * rows, hidden_width), BF16),
+            ((2, 2 * rows, hidden_width), BF16),
+            ((2, rows + down_rows, width), BF16),
+            ((2, rows + down_rows, width), BF16),
+            ((8, width), F32),
+        ],
+        [
+            ((QUERY_WIDTH, width), BF16),
+            ((hidden_width, width), BF16),
+            ((width, hidden_width), BF16),
+            ((width, hidden_width), BF16),
+            ((sequence, width), BF16),
+            ((sequence, width), BF16),
+            ((width, sequence), BF16),
+            ((sequence, hidden_width), BF16),
+            ((sequence, hidden_width), BF16),
+            ((sequence, hidden_width), BF16),
+            ((sequence, width), BF16),
+            ((width, hidden_width), BF16),
+            ((hidden_width, width), BF16),
+        ],
+        2 * sequence * width * (9 * hidden_width + 3 * QUERY_WIDTH),
+        sequence * hidden_width,
+        (place, x_seq, attended_t, dy_mine, dy_theirs, gains, *a_pieces, *b_pieces),
+        "feed_forward",
+    )
+    out_theirs = over_context(out_send)
+    gate_sum, up_sum = reduce_shard(keep_b, send_b, 0)
+    a_low, a_high = reduce_shard(keep_a, send_a, 0)
+    a_sum = jnp.concatenate([a_low, a_high], 0)
+
+    head_grads = []
+    for group in range(KEY_VALUE_HEADS):
+        head_grads += attend_back(group, qkv_t, log_total, attended_t, grad_t, cosine, sine)
+
+    keep_w, send_w, keep_x, send_x = call(
+        input_kernel,
+        [
+            ((2, rows, PACKED), BF16),
+            ((2, rows, PACKED), BF16),
+            ((half_rows, width), F32),
+            ((half_rows, width), BF16),
+        ],
+        [((PACKED, sequence), BF16), ((sequence, width), F32), ((width, PACKED), BF16)],
+        4 * sequence * width * PACKED,
+        sequence,
+        (place, x_seq, normed, packed_all, gains, gain2_grad, middle_grad, *head_grads),
+        "input_side",
+    )
+    x_theirs = over_context(send_x).astype(F32)
+    w_sum = jnp.concatenate(reduce_shard(keep_w, send_w, 1), 1)
+
+    def place_halves(keep, got):
+        return jnp.where(me == 0, jnp.stack([keep, got]), jnp.stack([got, keep]))
+
+    key_at = QUERY_WIDTH + KEY_WIDTH
+    value_at = key_at + KEY_WIDTH
+    return (
+        place_halves(out_keep, out_theirs),
+        place_halves(keep_x, x_theirs),
+        w_sum[:, value_at],
+        w_sum[:, :QUERY_WIDTH],
+        w_sum[:, QUERY_WIDTH:key_at],
+        w_sum[:, key_at:value_at],
+        a_sum[:rows],
+        w_sum[:, value_at + 1],
+        gate_sum,
+        up_sum,
+        a_sum[rows:],
+    )
+
+
+def layer_step(tokens, *rest):
+    whole = (
+        lax.axis_size("ctx") == 2
+        and lax.axis_size("fsdp") == 4
+        and lax.axis_size("dp") % 2 == 0
+        and tokens.shape[0] == 2
+        and tokens.shape[1] % TILE == 0
+    )
+    return (whole_sequences if whole else split_context)(tokens, *rest)
+
+
 def solution(mesh):
     return jax.shard_map(
-        local,
+        layer_step,
         mesh=mesh,
         in_specs=(
             P(("dp", "fsdp"), "ctx", None),

time: 649 us -> 287 us (0.44); the launches traced: 639 us -> 286 us
  blocking collectives: 150 us -> 0 us
  matrix products: 142 us -> 0 us
  waiting for transfers between devices: 253 us -> 111 us
  Pallas kernels: 0 us -> 91.6 us
  starting transfers between devices: 0.19 us -> 39.1 us
  local copies, waits for them, and re-layouts: 53.7 us -> 30.3 us
  between operations: 15.4 us -> 1.09 us
  other arithmetic: 23.2 us -> 13.2 us
    psum x1 -> x0, waiting for transfers between devices: 205 us -> none  [local(): lax.psum((grad_gain1, grad_query, grad_key, grad_value, grad_out, grad_ga...]
    dot_general x28 -> x0, matrix products: 142 us -> none  [the longest x2 18.1 us: block_scores(): jnp.einsum('gqhrd,gkhd->ghrqk', query_block, key_block, preferred_element...]
    ppermute x0 -> x34, waiting for transfers between devices: none -> 111 us  [the longest x10 41.6 us: over_context(): return lax.ppermute(tensor, 'ctx', [(0, 1), (1, 0)])]
    pallas_call x0 -> x6, Pallas kernels: none -> 91.6 us  [the longest x3 69.4 us: call(): pl.pallas_call(kernel, out_shape=shapes, in_specs=in_specs, out_specs=[pl...]
    psum x1 -> x0, blocking collectives: 88.5 us -> none  [local(): lax.psum((grad_gain1, grad_query, grad_key, grad_value, grad_out, grad_ga...]
    all_gather x6 -> x0, blocking collectives: 53.7 us -> none  [the longest x1 12.1 us: local(): lax.all_gather(key_local.reshape(query_group_count, local_row_count, key_...]
    reduce_scatter x1 -> x0, waiting for transfers between devices: 46.3 us -> none  [local(): lax.psum_scatter(terms.reshape(row_total, query_group_count, 2 * key_valu...]
    ppermute x0 -> x34, starting transfers between devices: none -> 39.1 us  [the longest x10 12.1 us: over_context(): return lax.ppermute(tensor, 'ctx', [(0, 1), (1, 0)])]
  transfers between devices with their start and end apart: 5 -> 34, of which waited for: 2 -> 16; matrix products, arithmetic and copies ran while one was open for 20% -> 13% of each run, Pallas kernels for 0% -> 8%
where the time goes in v1:
time: 287 us; the launch traced here: 286 us
  waiting for transfers between devices  111 us (39%)
  Pallas kernels  91.6 us (32%)
  starting transfers between devices  39.1 us (14%)
  local copies, waits for them, and re-layouts  30.3 us (11%)
  other arithmetic  13.2 us (5%)
    pallas_call x3, Pallas kernels, call(): pl.pallas_call(kernel, out_shape=shapes, in_specs=in_specs, out_specs=[pl...  69.4 us
    ppermute x10, waiting for transfers between devices, over_context(): return lax.ppermute(tensor, 'ctx', [(0, 1), (1, 0)])  41.6 us
    ppermute x15, waiting for transfers between devices, across(): return lax.ppermute(tensor, 'fsdp', [(i, i ^ bit) for i in range(4)])  40.5 us
    pallas_call x3, Pallas kernels, attend_back(): pl.pallas_call(attend_back_kernel, grid=(1,), out_shape=[jax.ShapeDtypeSt...  22.2 us
    ppermute x3, waiting for transfers between devices, sum_line(): got = lax.ppermute(part, 'dp', pairs)  21 us
    ppermute x10, starting transfers between devices, over_context(): return lax.ppermute(tensor, 'ctx', [(0, 1), (1, 0)])  12.1 us
    ppermute x15, starting transfers between devices, across(): return lax.ppermute(tensor, 'fsdp', [(i, i ^ bit) for i in range(4)])  11 us
    ppermute x3, starting transfers between devices, sum_line(): part = add(part, lax.ppermute(part, 'dp', pairs))  9.93 us
  transfers between devices with their start and end apart: 34, of which 16 were waited for; matrix products, arithmetic and copies ran while one was open for 13% of the time, Pallas kernels for 8%

profile of v1, /device:TPU:0, one launch (start us, length us, event | category | flops | bytes accessed | tf_op | source)
XLA Modules:
  0.0 286.2 jit_solution(13094374320901206340)
XLA Ops:
  3.4 3.0 %collective-permute-start.1 = (bf16[144,1024]{1,0:T(8,128)(2,1)S(1)}, bf16[144,1024]{1,0:T(8,128)(2,1)S(1)}, u32[]{:S(2)}, u32[]{:S(2)}) collective-permute-start(bf16[144,1024]{1,0:T(8,128)(2,1)S(1)} %concatenate.15.w_own), channel_id=1, source_target_pairs={{0,2},{1,3},{2,0},{3,1},{4,6},{5,7},{6,4},{7,5},{8,10},{9,11},{10,... | collective-permute-start | bytes 884744 | tf_op jit(solution)/shard_map/ppermute | solution.py:808
  9.1 4.4 %collective-permute-done.1.w_y = bf16[144,1024]{1,0:T(8,128)(2,1)S(1)} collective-permute-done((bf16[144,1024]{1,0:T(8,128)(2,1)S(1)}, bf16[144,1024]{1,0:T(8,128)(2,1)S(1)}, u32[]{:S(2)}, u32[]{:S(2)}) %collective-permute-start.1) | collective-permute-done | bytes 294944 | tf_op jit(solution)/shard_map/ppermute | solution.py:808
  20.1 10.2 %collective-permute-done = bf16[512,576]{0,1:T(8,128)(2,1)S(1)} collective-permute-done((bf16[512,576]{0,1:T(8,128)(2,1)}, bf16[512,576]{0,1:T(8,128)(2,1)S(1)}, u32[]{:S(2)}, u32[]{:S(2)}) %collective-permute-start) | collective-permute-done | bytes 589856 | tf_op jit(solution)/shard_map/ppermute | solution.py:812
  30.3 6.1 %collective-permute-done.8.b_y = bf16[288,1536]{1,0:T(8,128)(2,1)} collective-permute-done((bf16[288,1536]{1,0:T(8,128)(2,1)}, bf16[288,1536]{1,0:T(8,128)(2,1)}, u32[]{:S(2)}, u32[]{:S(2)}) %collective-permute-start.8) | collective-permute-done | bytes 884768 | tf_op jit(solution)/shard_map/ppermute | solution.py:808
  40.8 8.3 %collective-permute-done.5.a_y = bf16[528,576]{1,0:T(8,128)(2,1)} collective-permute-done((bf16[528,576]{1,0:T(8,128)(2,1)S(1)}, bf16[528,576]{1,0:T(8,128)(2,1)}, u32[]{:S(2)}, u32[]{:S(2)}) %collective-permute-start.5) | collective-permute-done | bytes 608288 | tf_op jit(solution)/shard_map/ppermute | solution.py:808
  53.2 23.1 %attend.1 = (bf16[1024,576]{1,0:T(8,128)(2,1)}, bf16[1024,576]{1,0:T(8,128)(2,1)}, bf16[576,1024]{1,0:T(8,128)(2,1)}, f32[8,576]{1,0:T(8,128)S(1)}, bf16[960,102...) custom-call(s32[2]{0:T(128)S(1)} %pad_add_fusion.place, bf16[512,576]{1,0:T(8,128)(2,1)} %bitcast.39, ...), custom_call_target="tpu_custom_call" | custom-call | flops 3623878656 | bytes 9422848 | tf_op jit(solution)/shard_map/attend/pallas_call | solution.py:753
  78.5 38.2 %feed_forward.1 = (bf16[512,576]{1,0:T(8,128)(2,1)S(1)}, bf16[512,576]{1,0:T(8,128)(2,1)S(1)}, f32[1024,576]{1,0:T(8,128)}, bf16[576,1024]{1,0:T(8,128)(2,1)}, b...) custom-call(s32[2]{0:T(128)S(1)} %pad_add_fusion.place, ...), custom_call_target="tpu_custom_call" | custom-call | flops 18345885696 | bytes 20238336 | tf_op jit(solution)/shard_map/feed_forward/pallas_call | solution.py:753
  116.7 7.3 %attend_back.5 = (bf16[192,1024]{1,0:T(8,128)(2,1)S(1)}, bf16[64,1024]{1,0:T(8,128)(2,1)S(1)}, bf16[64,1024]{1,0:T(8,128)(2,1)S(1)}) custom-call(bf16[960,1024]{1,0:T(8,128)(2,1)} %get-tuple-element.55.queries_t.keys_t.values_t, bf16[960,1024]{1,0:T(8,128)(2,1)} %get-tuple-element.55.queries_t.keys_t.values_t, ...), custom_call_target="tpu_custom_call" | custom-call | flops 2013265920 | bytes 4000000 | tf_op jit(solution)/shard_map/attend_back/pallas_call | solution.py:773
  124.1 7.3 %attend_back.4 = (bf16[192,1024]{1,0:T(8,128)(2,1)S(1)}, bf16[64,1024]{1,0:T(8,128)(2,1)S(1)}, bf16[64,1024]{1,0:T(8,128)(2,1)S(1)}) custom-call(bf16[960,1024]{1,0:T(8,128)(2,1)} %get-tuple-element.55.queries_t.keys_t.values_t, bf16[960,1024]{1,0:T(8,128)(2,1)} %get-tuple-element.55.queries_t.keys_t.values_t, ...), custom_call_target="tpu_custom_call" | custom-call | flops 2013265920 | bytes 4000000 | tf_op jit(solution)/shard_map/attend_back/pallas_call | solution.py:773
  131.4 7.6 %attend_back.3 = (bf16[192,1024]{1,0:T(8,128)(2,1)S(1)}, bf16[64,1024]{1,0:T(8,128)(2,1)S(1)}, bf16[64,1024]{1,0:T(8,128)(2,1)S(1)}) custom-call(bf16[960,1024]{1,0:T(8,128)(2,1)} %get-tuple-element.55.queries_t.keys_t.values_t, bf16[960,1024]{1,0:T(8,128)(2,1)} %get-tuple-element.55.queries_t.keys_t.values_t, ...), custom_call_target="tpu_custom_call" | custom-call | flops 2013265920 | bytes 4000000 | tf_op jit(solution)/shard_map/attend_back/pallas_call | solution.py:773
  139.0 8.1 %input_side.1 = (bf16[2,144,1024]{2,1,0:T(8,128)(2,1)}, bf16[2,144,1024]{2,1,0:T(8,128)(2,1)}, f32[512,576]{1,0:T(8,128)}, bf16[512,576]{1,0:T(8,128)(2,1)}) custom-call(s32[2]{0:T(128)S(1)} %pad_add_fusion.place, bf16[1024,576]{1,0:T(8,128)(2,1)} %get-tuple-element.43.x_seq, bf16[1024,576]{1,0:T(8,128)(2,1)} %get-tuple-element.51.normed, ...), custom_call_target="tpu_custom_call" | custom-call | flops 2415919104 | bytes 10850304 | tf_op jit(solution)/shard_map/input_side/pallas_call | solution.py:753
  154.7 10.5 %collective-permute-done.11 = bf16[512,576]{0,1:T(8,128)(2,1)} collective-permute-done((bf16[512,576]{0,1:T(8,128)(2,1)}, bf16[512,576]{0,1:T(8,128)(2,1)}, u32[]{:S(2)}, u32[]{:S(2)}) %collective-permute-start.11) | collective-permute-done | bytes 589856 | tf_op jit(solution)/shard_map/ppermute | solution.py:812
  168.3 8.6 %collective-permute-done.12 = bf16[512,576]{0,1:T(8,128)(2,1)} collective-permute-done((bf16[512,576]{0,1:T(8,128)(2,1)}, bf16[512,576]{0,1:T(8,128)(2,1)}, u32[]{:S(2)}, u32[]{:S(2)}) %collective-permute-start.12) | collective-permute-done | bytes 589856 | tf_op jit(solution)/shard_map/ppermute | solution.py:812
  179.9 3.6 %collective-permute-done.15 = bf16[144,512]{1,0:T(8,128)(2,1)S(1)} collective-permute-done((bf16[144,512]{1,0:T(8,128)(2,1)S(1)}, bf16[144,512]{1,0:T(8,128)(2,1)S(1)}, u32[]{:S(2)}, u32[]{:S(2)}) %collective-permute-start.15) | collective-permute-done | bytes 147488 | tf_op jit(solution)/shard_map/ppermute | solution.py:812
  184.3 4.0 %collective-permute-start.16 = (bf16[144,512]{1,0:T(8,128)(2,1)}, bf16[144,512]{1,0:T(8,128)(2,1)}, u32[]{:S(2)}, u32[]{:S(2)}) collective-permute-start(bf16[144,512]{1,0:T(8,128)(2,1)} %add_convert_fusion.11), channel_id=1, source_target_pairs={{0,8},{24,16},{1,9},{25,17},{2,10},{26,18},{3,11},{27,19},{4,12},{... | collective-permute-start | bytes 442376 | tf_op jit(solution)/shard_map/ppermute | solution.py:829
  200.6 9.0 %collective-permute-done.21 = bf16[528,576]{1,0:T(8,128)(2,1)} collective-permute-done((bf16[528,576]{1,0:T(8,128)(2,1)}, bf16[528,576]{1,0:T(8,128)(2,1)}, u32[]{:S(2)}, u32[]{:S(2)}) %collective-permute-start.21) | collective-permute-done | bytes 608288 | tf_op jit(solution)/shard_map/ppermute | solution.py:808
  212.7 12.6 %collective-permute-done.28 = bf16[288,1536]{1,0:T(8,128)(2,1)} collective-permute-done((bf16[288,1536]{1,0:T(8,128)(2,1)S(1)}, bf16[288,1536]{1,0:T(8,128)(2,1)}, u32[]{:S(2)}, u32[]{:S(2)}) %collective-permute-start.28) | collective-permute-done | bytes 884768 | tf_op jit(solution)/shard_map/ppermute | solution.py:808
  229.8 4.6 %collective-permute-start.23 = (bf16[264,576]{1,0:T(8,128)(2,1)S(1)}, bf16[264,576]{1,0:T(8,128)(2,1)S(1)}, u32[]{:S(2)}, u32[]{:S(2)}) collective-permute-start(bf16[264,576]{1,0:T(8,128)(2,1)S(1)} %add_convert_fusion.8), channel_id=1, source_target_pairs={{0,8},{24,16},{1,9},{25,17},{2,10},{26,18},{3,11},{27,19},{4,12},{... | collective-permute-start | bytes 912392 | tf_op jit(solution)/shard_map/ppermute | solution.py:829
  238.8 3.9 %collective-permute-done.23 = bf16[264,576]{1,0:T(8,128)(2,1)S(1)} collective-permute-done((bf16[264,576]{1,0:T(8,128)(2,1)S(1)}, bf16[264,576]{1,0:T(8,128)(2,1)S(1)}, u32[]{:S(2)}, u32[]{:S(2)}) %collective-permute-start.23) | collective-permute-done | bytes 304160 | tf_op jit(solution)/shard_map/ppermute | solution.py:829
  243.5 3.9 %collective-permute-done.30 = bf16[144,1536]{1,0:T(8,128)(2,1)S(1)} collective-permute-done((bf16[144,1536]{1,0:T(8,128)(2,1)S(1)}, bf16[144,1536]{1,0:T(8,128)(2,1)S(1)}, u32[]{:S(2)}, u32[]{:S(2)}) %collective-permute-start.30) | collective-permute-done | bytes 442400 | tf_op jit(solution)/shard_map/ppermute | solution.py:829
  252.6 15.4 %collective-permute-done.25 = bf16[264,576]{1,0:T(8,128)(2,1)S(1)} collective-permute-done((bf16[264,576]{1,0:T(8,128)(2,1)S(1)}, bf16[264,576]{1,0:T(8,128)(2,1)S(1)}, u32[]{:S(2)}, u32[]{:S(2)}) %collective-permute-start.25) | collective-permute-done | bytes 304160 | tf_op jit(solution)/shard_map/ppermute | solution.py:833
  268.3 5.6 %collective-permute-done.32 = bf16[144,1536]{1,0:T(8,128)(2,1)S(1)} collective-permute-done((bf16[144,1536]{1,0:T(8,128)(2,1)S(1)}, bf16[144,1536]{1,0:T(8,128)(2,1)S(1)}, u32[]{:S(2)}, u32[]{:S(2)}) %collective-permute-start.32) | collective-permute-done | bytes 442400 | tf_op jit(solution)/shard_map/ppermute | solution.py:833
  275.3 2.4 collective-permute-done.26
  279.8 5.0 %collective-permute-done.33 = bf16[144,1536]{1,0:T(8,128)(2,1)S(1)} collective-permute-done((bf16[144,1536]{1,0:T(8,128)(2,1)S(1)}, bf16[144,1536]{1,0:T(8,128)(2,1)S(1)}, u32[]{:S(2)}, u32[]{:S(2)}) %collective-permute-start.33) | collective-permute-done | bytes 442400 | tf_op jit(solution)/shard_map/ppermute | solution.py:812
  (136 shorter events, 72.2 us)
Async XLA Ops:
  13.5 22.9 %collective-permute-start.8 = (bf16[288,1536]{1,0:T(8,128)(2,1)}, bf16[288,1536]{1,0:T(8,128)(2,1)}, u32[]{:S(2)}, u32[]{:S(2)}) collective-permute-start(bf16[288,1536]{1,0:T(8,128)(2,1)} %constant_dynamic-update-slice_fusion.b_own), channel_id=1, source_target_pairs={{0,2},{1,3},{2,0},{3,1},{4,6},{5,7},{6,4},{7,5},{8,10},{9,11},{10,... | collective-permute-start | bytes 2654216 | tf_op jit(solution)/shard_map/ppermute | solution.py:808
  16.1 14.1 %collective-permute-start = (bf16[512,576]{0,1:T(8,128)(2,1)}, bf16[512,576]{0,1:T(8,128)(2,1)S(1)}, u32[]{:S(2)}, u32[]{:S(2)}) collective-permute-start(bf16[512,576]{0,1:T(8,128)(2,1)} %get-tuple-element.112), channel_id=1, source_target_pairs={{0,4},{4,0},{1,5},{5,1},{2,6},{6,2},{3,7},{7,3},{8,12},{12,8},{9,1... | collective-permute-start | bytes 1769480 | tf_op jit(solution)/shard_map/ppermute | solution.py:812
  19.0 30.1 %collective-permute-start.5 = (bf16[528,576]{1,0:T(8,128)(2,1)S(1)}, bf16[528,576]{1,0:T(8,128)(2,1)}, u32[]{:S(2)}, u32[]{:S(2)}) collective-permute-start(bf16[528,576]{1,0:T(8,128)(2,1)S(1)} %pad_maximum_fusion.1.a_own), channel_id=1, source_target_pairs={{0,2},{1,3},{2,0},{3,1},{4,6},{5,7},{6,4},{7,5},{8,10},{9,11},{10,... | collective-permute-start | bytes 1824776 | tf_op jit(solution)/shard_map/ppermute | solution.py:808
  19.5 19.0 %collective-permute-start.2 = (bf16[144,1024]{1,0:T(8,128)(2,1)S(1)}, bf16[144,1024]{1,0:T(8,128)(2,1)S(1)}, u32[]{:S(2)}, u32[]{:S(2)}) collective-permute-start(bf16[144,1024]{1,0:T(8,128)(2,1)S(1)} %concatenate.15.w_own), channel_id=1, source_target_pairs={{0,1},{1,0},{2,3},{3,2},{4,5},{5,4},{6,7},{7,6},{8,9},{9,8},{10,11... | collective-permute-start | bytes 884744 | tf_op jit(solution)/shard_map/ppermute | solution.py:808
  19.5 19.5 %collective-permute-start.3 = (bf16[144,1024]{1,0:T(8,128)(2,1)S(1)}, bf16[144,1024]{1,0:T(8,128)(2,1)S(1)}, u32[]{:S(2)}, u32[]{:S(2)}) collective-permute-start(bf16[144,1024]{1,0:T(8,128)(2,1)S(1)} %collective-permute-done.1.w_y), channel_id=1, source_target_pairs={{0,1},{1,0},{2,3},{3,2},{4,5},{5,4},{6,7},{7,6},{8,9},{9,8},{10,11... | collective-permute-start | bytes 884744 | tf_op jit(solution)/shard_map/ppermute | solution.py:808
  30.3 48.2 %collective-permute-start.9 = (bf16[288,1536]{1,0:T(8,128)(2,1)}, bf16[288,1536]{1,0:T(8,128)(2,1)}, u32[]{:S(2)}, u32[]{:S(2)}) collective-permute-start(bf16[288,1536]{1,0:T(8,128)(2,1)} %constant_dynamic-update-slice_fusion.b_own), channel_id=1, source_target_pairs={{0,1},{1,0},{2,3},{3,2},{4,5},{5,4},{6,7},{7,6},{8,9},{9,8},{10,11... | collective-permute-start | bytes 2654216 | tf_op jit(solution)/shard_map/ppermute | solution.py:808
  36.4 42.1 %collective-permute-start.10 = (bf16[288,1536]{1,0:T(8,128)(2,1)}, bf16[288,1536]{1,0:T(8,128)(2,1)}, u32[]{:S(2)}, u32[]{:S(2)}) collective-permute-start(bf16[288,1536]{1,0:T(8,128)(2,1)} %collective-permute-done.8.b_y), channel_id=1, source_target_pairs={{0,1},{1,0},{2,3},{3,2},{4,5},{5,4},{6,7},{7,6},{8,9},{9,8},{10,11... | collective-permute-start | bytes 2654216 | tf_op jit(solution)/shard_map/ppermute | solution.py:808
  38.6 39.9 %collective-permute-start.6 = (bf16[528,576]{1,0:T(8,128)(2,1)S(1)}, bf16[528,576]{1,0:T(8,128)(2,1)}, u32[]{:S(2)}, u32[]{:S(2)}) collective-permute-start(bf16[528,576]{1,0:T(8,128)(2,1)S(1)} %pad_maximum_fusion.1.a_own), channel_id=1, source_target_pairs={{0,1},{1,0},{2,3},{3,2},{4,5},{5,4},{6,7},{7,6},{8,9},{9,8},{10,11... | collective-permute-start | bytes 1824776 | tf_op jit(solution)/shard_map/ppermute | solution.py:808
  39.1 37.3 %collective-permute-start.4 = (bf16[512,576]{0,1:T(8,128)(2,1)}, bf16[512,576]{0,1:T(8,128)(2,1)}, u32[]{:S(2)}, u32[]{:S(2)}) collective-permute-start(bf16[512,576]{0,1:T(8,128)(2,1)} %get-tuple-element.45), channel_id=1, source_target_pairs={{0,4},{4,0},{1,5},{5,1},{2,6},{6,2},{3,7},{7,3},{8,12},{12,8},{9,1... | collective-permute-start | bytes 1769480 | tf_op jit(solution)/shard_map/ppermute | solution.py:812
  49.1 29.4 %collective-permute-start.7 = (bf16[528,576]{1,0:T(8,128)(2,1)}, bf16[528,576]{1,0:T(8,128)(2,1)}, u32[]{:S(2)}, u32[]{:S(2)}) collective-permute-start(bf16[528,576]{1,0:T(8,128)(2,1)} %collective-permute-done.5.a_y), channel_id=1, source_target_pairs={{0,1},{1,0},{2,3},{3,2},{4,5},{5,4},{6,7},{7,6},{8,9},{9,8},{10,11... | collective-permute-start | bytes 1824776 | tf_op jit(solution)/shard_map/ppermute | solution.py:808
  148.7 16.5 %collective-permute-start.11 = (bf16[512,576]{0,1:T(8,128)(2,1)}, bf16[512,576]{0,1:T(8,128)(2,1)}, u32[]{:S(2)}, u32[]{:S(2)}) collective-permute-start(bf16[512,576]{0,1:T(8,128)(2,1)} %copy.47), channel_id=1, source_target_pairs={{0,4},{4,0},{1,5},{5,1},{2,6},{6,2},{3,7},{7,3},{8,12},{12,8},{9,1... | collective-permute-start | bytes 1769480 | tf_op jit(solution)/shard_map/ppermute | solution.py:812
  151.2 25.7 %collective-permute-start.12 = (bf16[512,576]{0,1:T(8,128)(2,1)}, bf16[512,576]{0,1:T(8,128)(2,1)}, u32[]{:S(2)}, u32[]{:S(2)}) collective-permute-start(bf16[512,576]{0,1:T(8,128)(2,1)} %copy.49), channel_id=1, source_target_pairs={{0,4},{4,0},{1,5},{5,1},{2,6},{6,2},{3,7},{7,3},{8,12},{12,8},{9,1... | collective-permute-start | bytes 1769480 | tf_op jit(solution)/shard_map/ppermute | solution.py:812
  152.7 25.5 %collective-permute-start.14 = (bf16[144,1024]{1,0:T(8,128)(2,1)}, bf16[144,1024]{1,0:T(8,128)(2,1)S(1)}, u32[]{:S(2)}, u32[]{:S(2)}) collective-permute-start(bf16[144,1024]{1,0:T(8,128)(2,1)} %slice_bitcast_fusion.4), channel_id=1, source_target_pairs={{0,2},{1,3},{2,0},{3,1},{4,6},{5,7},{6,4},{7,5},{8,10},{9,11},{10,... | collective-permute-start | bytes 884744 | tf_op jit(solution)/shard_map/ppermute | solution.py:808
  154.2 34.2 %collective-permute-start.20 = (bf16[2,528,576]{2,1,0:T(8,128)(2,1)}, bf16[2,528,576]{2,1,0:T(8,128)(2,1)}, u32[]{:S(2)}, u32[]{:S(2)}) collective-permute-start(bf16[2,528,576]{2,1,0:T(8,128)(2,1)} %get-tuple-element.72), channel_id=1, source_target_pairs={{0,1},{1,0},{2,3},{3,2},{4,5},{5,4},{6,7},{7,6},{8,9},{9,8},{10,11... | collective-permute-start | bytes 3649544 | tf_op jit(solution)/shard_map/ppermute | solution.py:808
  154.2 38.5 %collective-permute-start.27 = (bf16[2,288,1536]{2,1,0:T(8,128)(2,1)}, bf16[2,288,1536]{2,1,0:T(8,128)(2,1)}, u32[]{:S(2)}, u32[]{:S(2)}) collective-permute-start(bf16[2,288,1536]{2,1,0:T(8,128)(2,1)} %get-tuple-element.74), channel_id=1, source_target_pairs={{0,1},{1,0},{2,3},{3,2},{4,5},{5,4},{6,7},{7,6},{8,9},{9,8},{10,11... | collective-permute-start | bytes 5308424 | tf_op jit(solution)/shard_map/ppermute | solution.py:808
  184.3 14.5 %collective-permute-start.16 = (bf16[144,512]{1,0:T(8,128)(2,1)}, bf16[144,512]{1,0:T(8,128)(2,1)}, u32[]{:S(2)}, u32[]{:S(2)}) collective-permute-start(bf16[144,512]{1,0:T(8,128)(2,1)} %add_convert_fusion.11), channel_id=1, source_target_pairs={{0,8},{24,16},{1,9},{25,17},{2,10},{26,18},{3,11},{27,19},{4,12},{... | collective-permute-start | bytes 442376 | tf_op jit(solution)/shard_map/ppermute | solution.py:829
  191.2 18.4 %collective-permute-start.21 = (bf16[528,576]{1,0:T(8,128)(2,1)}, bf16[528,576]{1,0:T(8,128)(2,1)}, u32[]{:S(2)}, u32[]{:S(2)}) collective-permute-start(bf16[528,576]{1,0:T(8,128)(2,1)} %slice_bitcast_fusion.2), channel_id=1, source_target_pairs={{0,2},{1,3},{2,0},{3,1},{4,6},{5,7},{6,4},{7,5},{8,10},{9,11},{10,... | collective-permute-start | bytes 1824776 | tf_op jit(solution)/shard_map/ppermute | solution.py:808
  194.7 30.5 %collective-permute-start.28 = (bf16[288,1536]{1,0:T(8,128)(2,1)S(1)}, bf16[288,1536]{1,0:T(8,128)(2,1)}, u32[]{:S(2)}, u32[]{:S(2)}) collective-permute-start(bf16[288,1536]{1,0:T(8,128)(2,1)S(1)} %slice_bitcast_fusion), channel_id=1, source_target_pairs={{0,2},{1,3},{2,0},{3,1},{4,6},{5,7},{6,4},{7,5},{8,10},{9,11},{10,... | collective-permute-start | bytes 2654216 | tf_op jit(solution)/shard_map/ppermute | solution.py:808
  199.8 28.5 %collective-permute-start.17 = (bf16[144,512]{1,0:T(8,128)(2,1)S(1)}, bf16[144,512]{1,0:T(8,128)(2,1)S(1)}, u32[]{:S(2)}, u32[]{:S(2)}) collective-permute-start(bf16[144,512]{1,0:T(8,128)(2,1)S(1)} %add_convert_fusion.10), channel_id=1, source_target_pairs={{8,16},{16,8},{9,17},{17,9},{10,18},{18,10},{11,19},{19,11},{12,20... | collective-permute-start | bytes 442376 | tf_op jit(solution)/shard_map/ppermute | solution.py:830
  211.1 18.5 %collective-permute-start.22 = (bf16[264,576]{1,0:T(8,128)(2,1)S(1)}, bf16[264,576]{1,0:T(8,128)(2,1)S(1)}, u32[]{:S(2)}, u32[]{:S(2)}) collective-permute-start(bf16[264,576]{1,0:T(8,128)(2,1)S(1)} %broadcast_select_fusion.3), channel_id=1, source_target_pairs={{0,4},{4,0},{1,5},{5,1},{2,6},{6,2},{3,7},{7,3},{8,12},{12,8},{9,1... | collective-permute-start | bytes 912392 | tf_op jit(solution)/shard_map/ppermute | solution.py:812
  229.8 12.9 %collective-permute-start.23 = (bf16[264,576]{1,0:T(8,128)(2,1)S(1)}, bf16[264,576]{1,0:T(8,128)(2,1)S(1)}, u32[]{:S(2)}, u32[]{:S(2)}) collective-permute-start(bf16[264,576]{1,0:T(8,128)(2,1)S(1)} %add_convert_fusion.8), channel_id=1, source_target_pairs={{0,8},{24,16},{1,9},{25,17},{2,10},{26,18},{3,11},{27,19},{4,12},{... | collective-permute-start | bytes 912392 | tf_op jit(solution)/shard_map/ppermute | solution.py:829
  235.8 11.6 %collective-permute-start.30 = (bf16[144,1536]{1,0:T(8,128)(2,1)S(1)}, bf16[144,1536]{1,0:T(8,128)(2,1)S(1)}, u32[]{:S(2)}, u32[]{:S(2)}) collective-permute-start(bf16[144,1536]{1,0:T(8,128)(2,1)S(1)} %add_convert_fusion.5), channel_id=1, source_target_pairs={{0,8},{24,16},{1,9},{25,17},{2,10},{26,18},{3,11},{27,19},{4,12},{... | collective-permute-start | bytes 1327112 | tf_op jit(solution)/shard_map/ppermute | solution.py:829
  249.1 18.9 %collective-permute-start.25 = (bf16[264,576]{1,0:T(8,128)(2,1)S(1)}, bf16[264,576]{1,0:T(8,128)(2,1)S(1)}, u32[]{:S(2)}, u32[]{:S(2)}) collective-permute-start(bf16[264,576]{1,0:T(8,128)(2,1)S(1)} %add_convert_fusion.6), channel_id=1, source_target_pairs={{8,0},{16,24},{9,1},{17,25},{10,2},{18,26},{11,3},{19,27},{12,4},{... | collective-permute-start | bytes 912392 | tf_op jit(solution)/shard_map/ppermute | solution.py:833
  250.6 23.3 %collective-permute-start.32 = (bf16[144,1536]{1,0:T(8,128)(2,1)S(1)}, bf16[144,1536]{1,0:T(8,128)(2,1)S(1)}, u32[]{:S(2)}, u32[]{:S(2)}) collective-permute-start(bf16[144,1536]{1,0:T(8,128)(2,1)S(1)} %add_convert_fusion.3), channel_id=1, source_target_pairs={{8,0},{16,24},{9,1},{17,25},{10,2},{18,26},{11,3},{19,27},{12,4},{... | collective-permute-start | bytes 1327112 | tf_op jit(solution)/shard_map/ppermute | solution.py:833
  (23 other events, 195.1 us)

commit v2 on v1

--- a/solution.py
+++ b/solution.py
@@ -404,10 +404,11 @@
 ROTATED = QUERY_HEADS + KEY_VALUE_HEADS
 REPEAT = QUERY_HEADS // KEY_VALUE_HEADS
 HALF = HEAD_SIZE // 2
-PACKED = QUERY_WIDTH + 2 * KEY_WIDTH + 64
-GAIN_AT = QUERY_WIDTH + 2 * KEY_WIDTH - (PACKED - 128)
+USED = QUERY_WIDTH + 2 * KEY_WIDTH
+PACKED = USED + 64
+GAIN_AT = USED - (PACKED - 128)
 TILE = 256
-VMEM_LIMIT = 52 * 1024 * 1024
+VMEM_LIMIT = 60 * 1024 * 1024
 F32 = jnp.float32
 BF16 = jnp.bfloat16
 
@@ -421,16 +422,42 @@
 
 
 def flip(tensor):
-    return tensor.astype(F32).T
-
-
-def rows_at(index, size):
-    return pl.ds(pl.multiple_of(index * size, size), size)
+    return tensor.astype(F32).T.astype(tensor.dtype)
+
+
+def span(index, size, step=None):
+    step = size if step is None else step
+    return pl.ds(pl.multiple_of(index * step, step), size)
+
+
+def flip_blocks(target, source, block):
+    def one(step, carry):
+        at = span(step, block)
+        target[at, :] = flip(source[:, at])
+        return carry
+
+    lax.fori_loop(0, source.shape[1] // block, one, 0)
+
+
+def column_scale(tensor):
+    return lax.rsqrt(jnp.mean(tensor * tensor, axis=0, keepdims=True) + EPSILON)
+
+
+def sigmoid(tensor):
+    return 0.5 * jnp.tanh(0.5 * tensor) + 0.5
+
+
+def causal_last(scores, tile):
+    visible = lax.broadcasted_iota(jnp.int32, (TILE, TILE), 0) <= lax.broadcasted_iota(
+        jnp.int32, (TILE, TILE), 1
+    )
+    last = jnp.where(visible, scores[tile * TILE :, :], MASKED)
+    return last if tile == 0 else jnp.concatenate([scores[: tile * TILE, :], last], 0)
 
 
 def attend_kernel(
     place,
-    mine,
+    tokens,
     theirs,
     w_own,
     w_y,
@@ -445,27 +472,27 @@
     qkv_t,
     log_total,
     attended_t,
+    packed_t,
     key_rows,
 ):
     me, shard = place[0], place[1]
-    half_rows = mine.shape[0]
+    half_rows = theirs.shape[1]
     sequence = 2 * half_rows
-    x_seq[rows_at(me, half_rows), :] = mine[...]
-    x_seq[rows_at(1 - me, half_rows), :] = theirs[...]
+    x_seq[:, span(me, half_rows)] = tokens[me]
+    x_seq[:, span(1 - me, half_rows)] = theirs[...]
     rows = w_own.shape[0]
     for bits, piece in ((0, w_own), (2, w_y), (1, w_core), (3, w_both)):
-        packed[rows_at(shard ^ bits, rows), :] = piece[...]
-    gain_rows = flip(packed[:, PACKED - 128 :])
-    gains[...] = gain_rows[GAIN_AT : GAIN_AT + 8, :]
-    gain1 = gain_rows[GAIN_AT : GAIN_AT + 1, :]
+        packed[span(shard ^ bits, rows), :] = piece[...]
+    flip_blocks(packed_t, packed, TILE)
+    gains[...] = packed[:, PACKED - 128 :].astype(F32)
+    gain1 = gains[:, GAIN_AT : GAIN_AT + 1]
 
     def project(tile, carry):
-        at = rows_at(tile, TILE)
-        x = x_seq[at, :].astype(F32)
-        scale = lax.rsqrt(jnp.mean(x * x, axis=-1, keepdims=True) + EPSILON)
-        normed_tile = (x * scale * gain1).astype(BF16)
-        normed[at, :] = normed_tile
-        turned = mm(normed_tile, packed[...]).T
+        at = span(tile, TILE)
+        x = x_seq[:, at].astype(F32)
+        normed_tile = (x * column_scale(x) * gain1).astype(BF16)
+        normed[:, at] = normed_tile
+        turned = mm(packed_t[:USED, :], normed_tile)
         cos, sin = cosine[:, at], sine[:, at]
         for head in range(ROTATED):
             a = turned[head * HEAD_SIZE : head * HEAD_SIZE + HALF, :]
@@ -476,26 +503,19 @@
             else:
                 key_rows[head - QUERY_HEADS, at, :] = both.T.astype(BF16)
             qkv_t[head * HEAD_SIZE : (head + 1) * HEAD_SIZE, at] = both.astype(BF16)
-        values = turned[ROTATED * HEAD_SIZE : ROTATED * HEAD_SIZE + KEY_WIDTH, :]
-        qkv_t[ROTATED * HEAD_SIZE :, at] = values.astype(BF16)
+        qkv_t[ROTATED * HEAD_SIZE :, at] = turned[ROTATED * HEAD_SIZE :, :].astype(BF16)
         return carry
 
     lax.fori_loop(0, sequence // TILE, project, 0)
 
     def one_head(head, carry):
         group = head // REPEAT
-        head_rows = rows_at(head, HEAD_SIZE)
-        value_rows = rows_at(ROTATED + group, HEAD_SIZE)
+        head_rows = span(head, HEAD_SIZE)
+        value_rows = span(ROTATED + group, HEAD_SIZE)
         for tile in range(sequence // TILE):
             extent = (tile + 1) * TILE
             cols = slice(tile * TILE, extent)
-            queries = qkv_t[head_rows, cols]
-            scores = mm(key_rows[group, :extent, :], queries)
-            visible = lax.broadcasted_iota(jnp.int32, (TILE, TILE), 0) <= lax.broadcasted_iota(
-                jnp.int32, (TILE, TILE), 1
-            )
-            last = jnp.where(visible, scores[tile * TILE :, :], MASKED)
-            scores = last if tile == 0 else jnp.concatenate([scores[: tile * TILE, :], last], 0)
+            scores = causal_last(mm(key_rows[group, :extent, :], qkv_t[head_rows, cols]), tile)
             top = jnp.max(scores, axis=0, keepdims=True)
             weights = jnp.exp(scores - top)
             total = jnp.sum(weights, axis=0, keepdims=True)
@@ -511,7 +531,7 @@
     place,
     x_seq,
     attended_t,
-    dy_mine,
+    out_grad,
     dy_theirs,
     gains,
     a_own,
@@ -532,92 +552,116 @@
     send_a,
     gain_grad,
     w_out,
-    w_down,
     w_gate,
     w_up,
+    w_down,
+    w_out_t,
+    w_gate_t,
+    w_up_t,
+    w_down_t,
     dy_seq,
-    out_seq,
     normed_t,
     hidden,
     gate_grad,
     up_grad,
     branch_grad,
+    gain_sum,
     total,
-    total_tall,
 ):
     me, shard = place[0], place[1]
-    half_rows = dy_mine.shape[0]
+    half_rows = dy_theirs.shape[1]
     sequence = 2 * half_rows
-    dy_seq[rows_at(me, half_rows), :] = dy_mine[...]
-    dy_seq[rows_at(1 - me, half_rows), :] = dy_theirs[...]
-    rows = b_own.shape[0] // 2
-    down_rows = a_own.shape[0] - rows
+    dy_seq[:, span(me, half_rows)] = out_grad[me]
+    dy_seq[:, span(1 - me, half_rows)] = dy_theirs[...]
+    rows = b_own.shape[0]
+    wide = w_gate.shape[1]
+    down_rows = a_own.shape[1]
     for bits, a, b in ((0, a_own, b_own), (2, a_y, b_y), (1, a_core, b_core), (3, a_both, b_both)):
-        w_out[rows_at(shard ^ bits, rows), :] = a[:rows, :]
-        w_down[rows_at(shard ^ bits, down_rows), :] = a[rows:, :]
-        w_gate[rows_at(shard ^ bits, rows), :] = b[:rows, :]
-        w_up[rows_at(shard ^ bits, rows), :] = b[rows:, :]
-    gain2 = gains[1:2, :]
-    gain_grad[...] = jnp.zeros_like(gain_grad)
+        at = span(shard ^ bits, rows)
+        w_gate[at, :] = b[:, :wide]
+        w_up[at, :] = b[:, wide : 2 * wide]
+        w_out[at, :] = b[:, 2 * wide :]
+        w_down_t[:, span(shard ^ bits, down_rows)] = a[...]
+    flip_blocks(w_gate_t, w_gate, TILE)
+    flip_blocks(w_up_t, w_up, TILE)
+    w_out_t[...] = flip(w_out[...])
+    flip_blocks(w_down, w_down_t, TILE)
+    gain2 = gains[:, GAIN_AT + 1 : GAIN_AT + 2]
+    gain_sum[...] = jnp.zeros_like(gain_sum)
 
     def one_tile(tile, carry):
-        at = rows_at(tile, TILE)
-        attended = flip(attended_t[:, at]).astype(BF16)
-        middle = x_seq[at, :].astype(F32) + mm(attended, w_out[...])
-        scale = lax.rsqrt(jnp.mean(middle * middle, axis=-1, keepdims=True) + EPSILON)
+        at = span(tile, TILE)
+        middle = x_seq[:, at].astype(F32) + mm(w_out_t[...], attended_t[:, at])
+        scale = column_scale(middle)
         ready = middle * scale
-        normed = ready * gain2
-        normed_t[:, at] = normed.T.astype(BF16)
-        normed = normed.astype(BF16)
-        gate = mm(normed, w_gate[...])
-        up = mm(normed, w_up[...])
-        sig = 1.0 / (1.0 + jnp.exp(-gate))
+        normed = (ready * gain2).astype(BF16)
+        normed_t[:, at] = normed
+        gate = mm(w_gate_t[...], normed)
+        up = mm(w_up_t[...], normed)
+        sig = sigmoid(gate)
         silu = gate * sig
         hidden_tile = (silu * up).astype(BF16)
-        hidden[at, :] = hidden_tile
-        out_seq[at, :] = (middle + mm(hidden_tile, w_down[...])).astype(BF16)
-        dy = dy_seq[at, :]
-        hidden_grad = mm_nt(dy, w_down[...])
+        hidden[:, at] = hidden_tile
+        output = (middle + mm(w_down_t[...], hidden_tile)).astype(BF16)
+        block = tile // (half_rows // TILE)
+        block_cols = span(tile - block * (half_rows // TILE), TILE)
+
+        @pl.when(block == me)
+        def _():
+            out_keep[:, block_cols] = output
+
+        @pl.when(block != me)
+        def _():
+            out_send[:, block_cols] = output
+
+        dy = dy_seq[:, at]
+        hidden_grad = mm(w_down[...], dy)
         gate_tile = (hidden_grad * up * sig * (1.0 + gate * (1.0 - sig))).astype(BF16)
         up_tile = (hidden_grad * silu).astype(BF16)
-        gate_grad[at, :] = gate_tile
-        up_grad[at, :] = up_tile
-        normed_grad = mm_nt(gate_tile, w_gate[...]) + mm_nt(up_tile, w_up[...])
-        gain_grad[0:1, :] += jnp.sum(normed_grad * ready, axis=0, keepdims=True)
+        gate_grad[:, at] = gate_tile
+        up_grad[:, at] = up_tile
+        normed_grad = mm(w_gate[...], gate_tile) + mm(w_up[...], up_tile)
+        gain_sum[...] += normed_grad * ready
         scaled = normed_grad * gain2
         middle_grad = (
             dy.astype(F32)
             + scale * scaled
-            - middle * (scale * scale * scale) * jnp.mean(scaled * middle, axis=-1, keepdims=True)
+            - middle * (scale * scale * scale) * jnp.mean(scaled * middle, axis=0, keepdims=True)
         )
-        middle_grad_out[at, :] = middle_grad
+        middle_grad_out[:, at] = middle_grad
         branch = middle_grad.astype(BF16)
-        branch_grad[at, :] = branch
-        attended_grad_t[:, at] = mm_nt(branch, w_out[...]).T.astype(BF16)
+        branch_grad[:, at] = branch
+        attended_grad_t[:, at] = mm(w_out[...], branch).astype(BF16)
         return carry
 
     lax.fori_loop(0, sequence // TILE, one_tile, 0)
-    out_keep[...] = out_seq[rows_at(me, half_rows), :]
-    out_send[...] = out_seq[rows_at(1 - me, half_rows), :]
-    wide = gate_grad.shape[1]
-    for part, grads in ((0, gate_grad), (1, up_grad)):
-        for first in range(0, wide, 512):
-            cols = slice(first, min(first + 512, wide))
-            total[:, cols] = mm(normed_t[...], grads[:, cols]).astype(BF16)
-        at = slice(part * rows, (part + 1) * rows)
-        for y_bit in range(2):
-            keep_b[y_bit, at, :] = total[rows_at(shard ^ (2 * y_bit), rows), :]
-            send_b[y_bit, at, :] = total[rows_at(shard ^ (2 * y_bit + 1), rows), :]
-    for first in range(0, wide, 512):
-        cols = slice(first, min(first + 512, wide))
-        total_tall[cols, :] = mm(flip(hidden[:, cols]).astype(BF16), dy_seq[...]).astype(BF16)
+    gain_grad[...] = jnp.broadcast_to(
+        jnp.sum(gain_sum[...], axis=1, keepdims=True), gain_grad.shape
+    )
+
+    half = rows // 2
+    for left, right, first in (
+        (normed_t, gate_grad, 0),
+        (normed_t, up_grad, wide),
+        (attended_t, branch_grad, 2 * wide),
+    ):
+        size = right.shape[0]
+        for start in range(0, size, 512):
+            count = min(512, size - start)
+            total[:, :count] = mm_nt(left[...], right[start : start + count, :])
+            cols = slice(first + start, first + start + count)
+            for y_bit in range(2):
+                for x_bit in range(2):
+                    for core_bit, target in ((0, keep_b), (1, send_b)):
+                        row = (shard ^ (2 * y_bit + core_bit)) * 2 + (me ^ x_bit)
+                        target[y_bit, x_bit, :, cols] = total[span(row, half), :count].astype(BF16)
+    half = keep_a.shape[2]
     for y_bit in range(2):
-        keep_a[y_bit, rows:, :] = total_tall[rows_at(shard ^ (2 * y_bit), down_rows), :]
-        send_a[y_bit, rows:, :] = total_tall[rows_at(shard ^ (2 * y_bit + 1), down_rows), :]
-    total[:, :QUERY_WIDTH] = mm(attended_t[...], branch_grad[...]).astype(BF16)
-    for y_bit in range(2):
-        keep_a[y_bit, :rows, :] = total[rows_at(shard ^ (2 * y_bit), rows), :QUERY_WIDTH]
-        send_a[y_bit, :rows, :] = total[rows_at(shard ^ (2 * y_bit + 1), rows), :QUERY_WIDTH]
+        for core_bit, target in ((0, keep_a), (1, send_a)):
+            columns = span(shard ^ (2 * y_bit + core_bit), down_rows)
+            total[:, :down_rows] = mm_nt(dy_seq[...], hidden[columns, :])
+            for x_bit in range(2):
+                target[x_bit, y_bit] = total[span(me ^ x_bit, half), :down_rows].astype(BF16)
 
 
 def attend_back_kernel(
@@ -639,8 +683,8 @@
     dq,
 ):
     sequence = keys_t.shape[1]
-    keys[...] = flip(keys_t[...]).astype(BF16)
-    values[...] = flip(values_t[...]).astype(BF16)
+    keys[...] = flip(keys_t[...])
+    values[...] = flip(values_t[...])
     dk[...] = jnp.zeros_like(dk)
     dv[...] = jnp.zeros_like(dv)
 
@@ -648,7 +692,7 @@
         return (a * cos + b * sin).astype(BF16), (b * cos - a * sin).astype(BF16)
 
     def one_head(head, carry):
-        head_rows = rows_at(head, HEAD_SIZE)
+        head_rows = span(head, HEAD_SIZE)
         for tile in range(sequence // TILE):
             extent = (tile + 1) * TILE
             cols = slice(tile * TILE, extent)
@@ -658,22 +702,17 @@
             delta = jnp.sum(
                 do_wide * attended_t[head_rows, cols].astype(F32), axis=0, keepdims=True
             )
-            scores = mm(keys[:extent, :], q_t)
-            visible = lax.broadcasted_iota(jnp.int32, (TILE, TILE), 0) <= lax.broadcasted_iota(
-                jnp.int32, (TILE, TILE), 1
-            )
-            last = jnp.where(visible, scores[tile * TILE :, :], MASKED)
-            scores = last if tile == 0 else jnp.concatenate([scores[: tile * TILE, :], last], 0)
+            scores = causal_last(mm(keys[:extent, :], q_t), tile)
             probs = jnp.exp(scores - log_total[0, pl.ds(head, 1), cols])
             dprob = mm(values[:extent, :], do_t)
             score_grad = (probs * (dprob - delta)).astype(BF16)
             dv[:extent, :] += mm(probs.astype(BF16), do_wide.T.astype(BF16))
-            dk[:extent, :] += mm(score_grad, flip(q_t).astype(BF16))
+            dk[:extent, :] += mm(score_grad, flip(q_t))
             dq[:, cols] = mm(keys_t[:, :extent], score_grad) * 0.125
         cos, sin = cosine[...], sine[...]
         a, b = back(dq[:HALF, :], dq[HALF:, :], cos, sin)
-        dq_out[pl.ds(pl.multiple_of(head * HEAD_SIZE, HEAD_SIZE), HALF), :] = a
-        dq_out[pl.ds(pl.multiple_of(head * HEAD_SIZE + HALF, HALF), HALF), :] = b
+        dq_out[span(head, HALF, HEAD_SIZE), :] = a
+        dq_out[span(2 * head + 1, HALF), :] = b
         return carry
 
     lax.fori_loop(0, queries_t.shape[0] // HEAD_SIZE, one_head, 0)
@@ -684,20 +723,11 @@
     dv_out[...] = dv[...].T.astype(BF16)
 
 
-def input_kernel(
-    place,
-    x_seq,
-    normed,
-    packed,
-    gains,
-    gain2_grad,
-    middle_grad,
-    *rest,
-):
+def input_kernel(place, x_seq, normed, packed, gains, gain2_grad, middle_grad, *rest):
     heads = rest[: 3 * KEY_VALUE_HEADS]
     keep_w, send_w, keep_x, send_x, joined, grad_seq, total = rest[3 * KEY_VALUE_HEADS :]
     me, shard = place[0], place[1]
-    half_rows = keep_x.shape[0]
+    half_rows = keep_x.shape[1]
     sequence = 2 * half_rows
     group_width = REPEAT * HEAD_SIZE
     for group in range(KEY_VALUE_HEADS):
@@ -707,39 +737,36 @@
         joined[at : at + HEAD_SIZE, :] = dk[...]
         at = QUERY_WIDTH + KEY_WIDTH + group * HEAD_SIZE
         joined[at : at + HEAD_SIZE, :] = dv[...]
-    joined[QUERY_WIDTH + 2 * KEY_WIDTH :, :] = jnp.zeros(
-        (PACKED - QUERY_WIDTH - 2 * KEY_WIDTH, sequence), BF16
-    )
-    gain1 = gains[0:1, :]
-    gain1_grad = jnp.zeros((1, WIDTH), F32)
+    joined[USED:, :] = jnp.zeros((PACKED - USED, sequence), BF16)
+    gain1 = gains[:, GAIN_AT : GAIN_AT + 1]
+    gain_sum = jnp.zeros((WIDTH, TILE), F32)
     for tile in range(sequence // TILE):
         at = slice(tile * TILE, (tile + 1) * TILE)
-        normed_grad = mm(packed[...], joined[:, at]).T
-        x = x_seq[at, :].astype(F32)
-        scale = lax.rsqrt(jnp.mean(x * x, axis=-1, keepdims=True) + EPSILON)
-        gain1_grad += jnp.sum(normed_grad * x * scale, axis=0, keepdims=True)
+        normed_grad = mm(packed[...], joined[:, at])
+        x = x_seq[:, at].astype(F32)
+        scale = column_scale(x)
+        gain_sum += normed_grad * x * scale
         scaled = normed_grad * gain1
-        grad_seq[at, :] = (
-            middle_grad[at, :]
+        grad_seq[:, at] = (
+            middle_grad[:, at]
             + scale * scaled
-            - x * (scale * scale * scale) * jnp.mean(scaled * x, axis=-1, keepdims=True)
+            - x * (scale * scale * scale) * jnp.mean(scaled * x, axis=0, keepdims=True)
         )
-    keep_x[...] = grad_seq[rows_at(me, half_rows), :]
-    send_x[...] = grad_seq[rows_at(1 - me, half_rows), :].astype(BF16)
-    for first in range(0, PACKED, TILE):
-        at = slice(first, first + TILE)
-        total[:, at] = mm(joined[at, :], normed[...]).T.astype(BF16)
-    row = lax.broadcasted_iota(jnp.int32, (128, WIDTH), 0)
-    gain_rows = jnp.where(row == GAIN_AT, gain1_grad, 0.0) + jnp.where(
-        row == GAIN_AT + 1, gain2_grad[0:1, :], 0.0
-    )
+    keep_x[...] = grad_seq[:, span(me, half_rows)]
+    send_x[...] = grad_seq[:, span(1 - me, half_rows)].astype(BF16)
+    for first in range(0, PACKED, 512):
+        total[:, first : first + 512] = mm_nt(normed[...], joined[first : first + 512, :])
     lane = lax.broadcasted_iota(jnp.int32, (WIDTH, 128), 1)
-    last = total[:, PACKED - 128 :].astype(F32)
-    total[:, PACKED - 128 :] = jnp.where(lane < GAIN_AT, last, gain_rows.T).astype(BF16)
-    rows = keep_w.shape[1]
+    last = total[:, PACKED - 128 :]
+    last = jnp.where(lane == GAIN_AT, jnp.sum(gain_sum, axis=1, keepdims=True), last)
+    total[:, PACKED - 128 :] = jnp.where(lane == GAIN_AT + 1, gain2_grad[...], last)
+    half = keep_w.shape[2]
     for y_bit in range(2):
-        keep_w[y_bit] = total[rows_at(shard ^ (2 * y_bit), rows), :]
-        send_w[y_bit] = total[rows_at(shard ^ (2 * y_bit + 1), rows), :]
+        for x_bit in range(2):
+            row = (shard ^ (2 * y_bit)) * 2 + (me ^ x_bit)
+            keep_w[y_bit, x_bit] = total[span(row, half), :].astype(BF16)
+            row = (shard ^ (2 * y_bit + 1)) * 2 + (me ^ x_bit)
+            send_w[y_bit, x_bit] = total[span(row, half), :].astype(BF16)
 
 
 def call(kernel, out, scratch, flops, exps, args, name):
@@ -816,6 +843,10 @@
     return lax.optimization_barrier((tensor, *done))[0]
 
 
+def together(*values):
+    return lax.optimization_barrier(values)
+
+
 def add(a, b):
     return (a.astype(F32) + b.astype(F32)).astype(BF16)
 
@@ -835,26 +866,6 @@
     return part
 
 
-def reduce_shard(keep, send, axis):
-    me = lax.axis_index("ctx")
-    pair = add(keep, across(send, 1))
-    own = add(pair[0], across(pair[1], 2))
-    low, high = jnp.split(own, 2, axis)
-    part = add(jnp.where(me == 0, low, high), over_context(jnp.where(me == 0, high, low)))
-    part = sum_line(part)
-    other = over_context(part)
-    return (
-        jnp.where(me == 0, part, other).astype(F32),
-        jnp.where(me == 0, other, part).astype(F32),
-    )
-
-
-def gather_pieces(own, *done):
-    first = after(own, *done) if done else own
-    y_piece = across(first, 2)
-    return own, y_piece, across(first, 1), across(y_piece, 1)
-
-
 def whole_sequences(
     tokens, norm1_gain, w_query, w_key, w_value, w_out, norm2_gain, w_gate, w_up, w_down, out_grad
 ):
@@ -865,6 +876,8 @@
     hidden_width = w_gate.shape[1]
     me = lax.axis_index("ctx")
     place = jnp.stack([me, lax.axis_index("fsdp")]).astype(jnp.int32)
+    tokens = jnp.swapaxes(tokens, 1, 2)
+    out_grad = jnp.swapaxes(out_grad, 1, 2)
 
     packed = jnp.concatenate(
         [
@@ -873,16 +886,19 @@
             w_value,
             norm1_gain[:, None],
             norm2_gain[:, None],
-            jnp.zeros((rows, PACKED - QUERY_WIDTH - 2 * KEY_WIDTH - 2), BF16),
+            jnp.zeros((rows, PACKED - USED - 2), BF16),
         ],
         1,
     )
-    packed_pieces = gather_pieces(packed)
-    tokens_mine = lax.dynamic_index_in_dim(tokens, me, 0, False)
     tokens_theirs = over_context(lax.dynamic_index_in_dim(tokens, 1 - me, 0, False))
-    a_pieces = gather_pieces(jnp.concatenate([w_out, w_down], 0), packed_pieces[1])
-    b_pieces = gather_pieces(jnp.concatenate([w_gate, w_up], 0), packed_pieces[1])
-    dy_mine = lax.dynamic_index_in_dim(out_grad, me, 0, False)
+    packed_y = across(packed, 2)
+    packed_core = across(packed, 1)
+    packed_both = across(packed_y, 1)
+    b_own = jnp.concatenate([w_gate, w_up, w_out], 1)
+    a_own = w_down.T
+    b_own, a_own = together(b_own, a_own, packed_y)[:2]
+    b_y, a_y = across(b_own, 2), across(a_own, 2)
+    b_core, a_core = across(b_own, 1), across(a_own, 1)
     dy_theirs = over_context(
         after(lax.dynamic_index_in_dim(out_grad, 1 - me, 0, False), tokens_theirs)
     )
@@ -894,21 +910,28 @@
     x_seq, normed, packed_all, gains, qkv_t, log_total, attended_t = call(
         attend_kernel,
         [
-            ((sequence, width), BF16),
-            ((sequence, width), BF16),
+            ((width, sequence), BF16),
+            ((width, sequence), BF16),
             ((width, PACKED), BF16),
-            ((8, width), F32),
-            ((QUERY_WIDTH + 2 * KEY_WIDTH, sequence), BF16),
+            ((width, 128), F32),
+            ((USED, sequence), BF16),
             ((KEY_VALUE_HEADS, 8, sequence), F32),
             ((QUERY_WIDTH, sequence), BF16),
         ],
-        [((KEY_VALUE_HEADS, sequence, HEAD_SIZE), BF16)],
+        [((PACKED, width), BF16), ((KEY_VALUE_HEADS, sequence, HEAD_SIZE), BF16)],
         2 * sequence * width * PACKED + 4 * QUERY_WIDTH * pairs,
         QUERY_HEADS * pairs,
-        (place, tokens_mine, tokens_theirs, *packed_pieces, cosine, sine),
+        (place, tokens, tokens_theirs, packed, packed_y, packed_core, packed_both, cosine, sine),
         "attend",
     )
 
+    b_y, a_y, b_core, a_core, dy_theirs, attended_t = together(
+        b_y, a_y, b_core, a_core, dy_theirs, attended_t
+    )
+    b_both, a_both = across(b_y, 1), across(a_y, 1)
+
+    b_shape = ((2, 2, rows // 2, b_own.shape[1]), BF16)
+    a_shape = ((2, 2, width // 2, down_rows), BF16)
     (
         out_keep,
         out_send,
@@ -922,79 +945,134 @@
     ) = call(
         feed_forward_kernel,
         [
-            ((half_rows, width), BF16),
-            ((half_rows, width), BF16),
-            ((sequence, width), F32),
+            ((width, half_rows), BF16),
+            ((width, half_rows), BF16),
+            ((width, sequence), F32),
             ((QUERY_WIDTH, sequence), BF16),
-            ((2, 2 * rows, hidden_width), BF16),
-            ((2, 2 * rows, hidden_width), BF16),
-            ((2, rows + down_rows, width), BF16),
-            ((2, rows + down_rows, width), BF16),
-            ((8, width), F32),
+            b_shape,
+            b_shape,
+            a_shape,
+            a_shape,
+            ((width, 128), F32),
         ],
         [
             ((QUERY_WIDTH, width), BF16),
+            ((width, hidden_width), BF16),
+            ((width, hidden_width), BF16),
+            ((hidden_width, width), BF16),
+            ((width, QUERY_WIDTH), BF16),
+            ((hidden_width, width), BF16),
             ((hidden_width, width), BF16),
             ((width, hidden_width), BF16),
-            ((width, hidden_width), BF16),
-            ((sequence, width), BF16),
-            ((sequence, width), BF16),
             ((width, sequence), BF16),
-            ((sequence, hidden_width), BF16),
-            ((sequence, hidden_width), BF16),
-            ((sequence, hidden_width), BF16),
-            ((sequence, width), BF16),
-            ((width, hidden_width), BF16),
-            ((hidden_width, width), BF16),
+            ((width, sequence), BF16),
+            ((hidden_width, sequence), BF16),
+            ((hidden_width, sequence), BF16),
+            ((hidden_width, sequence), BF16),
+            ((width, sequence), BF16),
+            ((width, TILE), F32),
+            ((width, 512), F32),
         ],
         2 * sequence * width * (9 * hidden_width + 3 * QUERY_WIDTH),
         sequence * hidden_width,
-        (place, x_seq, attended_t, dy_mine, dy_theirs, gains, *a_pieces, *b_pieces),
+        (
+            place,
+            x_seq,
+            attended_t,
+            out_grad,
+            dy_theirs,
+            gains,
+            a_own,
+            a_y,
+            a_core,
+            a_both,
+            b_own,
+            b_y,
+            b_core,
+            b_both,
+        ),
         "feed_forward",
     )
+
+    back_args = (log_total, attended_t, grad_t, cosine, sine)
     out_theirs = over_context(out_send)
-    gate_sum, up_sum = reduce_shard(keep_b, send_b, 0)
-    a_low, a_high = reduce_shard(keep_a, send_a, 0)
-    a_sum = jnp.concatenate([a_low, a_high], 0)
-
-    head_grads = []
-    for group in range(KEY_VALUE_HEADS):
-        head_grads += attend_back(group, qkv_t, log_total, attended_t, grad_t, cosine, sine)
+    got_b, got_a = across(send_b, 1), across(send_a, 1)
+    grads0 = attend_back(0, qkv_t, *back_args)
+    got_b, got_a, *grads0 = together(got_b, got_a, *grads0)
+    b0, b1 = add(keep_b[0], got_b[0]), add(keep_b[1], got_b[1])
+    a0, a1 = add(keep_a[0], got_a[0]), add(keep_a[1], got_a[1])
+    b1, a1, qkv_t = together(b1, a1, qkv_t)
+    got_b, got_a = across(b1, 2), over_context(a1)
+    grads1 = attend_back(1, qkv_t, *back_args)
+    grads2 = attend_back(2, qkv_t, *back_args)
+    got_b, got_a, out_theirs, *grads2 = together(got_b, got_a, out_theirs, *grads2)
+    b0, b1 = add(b0[0], got_b[0]), add(b0[1], got_b[1])
+    a0, a1 = add(a0[0], got_a[0]), add(a0[1], got_a[1])
+    b1, a1, *grads2 = together(b1, a1, *grads2)
+    got_b, got_a = over_context(b1), across(a1, 2)
 
     keep_w, send_w, keep_x, send_x = call(
         input_kernel,
         [
-            ((2, rows, PACKED), BF16),
-            ((2, rows, PACKED), BF16),
-            ((half_rows, width), F32),
-            ((half_rows, width), BF16),
+            ((2, 2, rows // 2, PACKED), BF16),
+            ((2, 2, rows // 2, PACKED), BF16),
+            ((width, half_rows), F32),
+            ((width, half_rows), BF16),
         ],
-        [((PACKED, sequence), BF16), ((sequence, width), F32), ((width, PACKED), BF16)],
+        [((PACKED, sequence), BF16), ((width, sequence), F32), ((width, PACKED), F32)],
         4 * sequence * width * PACKED,
         sequence,
-        (place, x_seq, normed, packed_all, gains, gain2_grad, middle_grad, *head_grads),
+        (
+            place,
+            x_seq,
+            normed,
+            packed_all,
+            gains,
+            gain2_grad,
+            middle_grad,
+            *grads0,
+            *grads1,
+            *grads2,
+        ),
         "input_side",
     )
-    x_theirs = over_context(send_x).astype(F32)
-    w_sum = jnp.concatenate(reduce_shard(keep_w, send_w, 1), 1)
+    got_b, got_a, send_w = together(got_b, got_a, send_w)
+    w_got = across(send_w, 1)
+    x_theirs = over_context(send_x)
+    b_part = sum_line(add(b0, got_b))
+    a_part = sum_line(add(a0, got_a))
+    w0, w1 = add(keep_w[0], w_got[0]), add(keep_w[1], w_got[1])
+    w_got = across(w1, 2)
+    w0, w1 = add(w0[0], w_got[0]), add(w0[1], w_got[1])
+    w_part = sum_line(add(w0, over_context(w1)))
+
+    def both_halves(part, other):
+        first = jnp.where(me == 0, part, other)
+        second = jnp.where(me == 0, other, part)
+        return jnp.concatenate([first, second], 0).astype(F32)
+
+    b_sum = both_halves(b_part, over_context(b_part))
+    a_sum = both_halves(a_part, over_context(a_part))
+    w_sum = both_halves(w_part, over_context(w_part))
 
     def place_halves(keep, got):
-        return jnp.where(me == 0, jnp.stack([keep, got]), jnp.stack([got, keep]))
+        got = got.astype(keep.dtype)
+        both = jnp.where(me == 0, jnp.stack([keep, got]), jnp.stack([got, keep]))
+        return jnp.swapaxes(both, 1, 2)
 
     key_at = QUERY_WIDTH + KEY_WIDTH
-    value_at = key_at + KEY_WIDTH
     return (
         place_halves(out_keep, out_theirs),
         place_halves(keep_x, x_theirs),
-        w_sum[:, value_at],
+        w_sum[:, USED],
         w_sum[:, :QUERY_WIDTH],
         w_sum[:, QUERY_WIDTH:key_at],
-        w_sum[:, key_at:value_at],
-        a_sum[:rows],
-        w_sum[:, value_at + 1],
-        gate_sum,
-        up_sum,
-        a_sum[rows:],
+        w_sum[:, key_at:USED],
+        b_sum[:, 2 * hidden_width :],
+        w_sum[:, USED + 1],
+        b_sum[:, :hidden_width],
+        b_sum[:, hidden_width : 2 * hidden_width],
+        a_sum.T,
     )
 
 

time: 287 us -> 238 us (0.83)
  waiting for transfers between devices: 111 us -> 64.9 us
  local copies, waits for them, and re-layouts: 30.3 us -> 9.45 us
  Pallas kernels: 91.6 us -> 103 us
  other arithmetic: 13.2 us -> 19.7 us
    ppermute x15, waiting for transfers between devices: 40.5 us -> 11.6 us  [across(): return lax.ppermute(tensor, 'fsdp', [(i, i ^ bit) for i in range(4)])]
    pallas_call x3, Pallas kernels: 69.4 us -> 78.5 us  [call(): pl.pallas_call(kernel, out_shape=shapes, in_specs=in_specs, out_specs=[pl...]
    ppermute x10, waiting for transfers between devices: 41.6 us -> 33.7 us  [over_context(): return lax.ppermute(tensor, 'ctx', [(0, 1), (1, 0)])]
    ppermute x4 -> x0, local copies, waits for them, and re-layouts: 6.99 us -> none  [over_context(): return lax.ppermute(tensor, 'ctx', [(0, 1), (1, 0)])]
    unnamed x31 -> x42, local copies, waits for them, and re-layouts: 9.07 us -> 2.98 us
    ppermute x3, waiting for transfers between devices: 21 us -> 15.1 us  [sum_line(): got = lax.ppermute(part, 'dp', pairs)]
    transpose x0 -> x3, other arithmetic: none -> 5.13 us  [the longest x2 4.16 us: place_halves(): return jnp.swapaxes(both, 1, 2)]
    ppermute x3, waiting for transfers between devices: 7.86 us -> 4.47 us  [sum_line(): part = add(part, lax.ppermute(part, 'dp', pairs))]
  transfers between devices with their start and end apart: 34 -> 34, of which waited for: 16 -> 14; matrix products, arithmetic and copies ran while one was open for 13% -> 6% of each run, Pallas kernels for 8% -> 24%
where the time goes in v2:
time: 238 us; the launch traced here: 237 us
  Pallas kernels  103 us (43%)
  waiting for transfers between devices  64.9 us (27%)
  starting transfers between devices  38.7 us (16%)
  other arithmetic  19.7 us (8%)
  local copies, waits for them, and re-layouts  9.45 us (4%)
    pallas_call x3, Pallas kernels, call(): pl.pallas_call(kernel, out_shape=shapes, in_specs=in_specs, out_specs=[pl...  78.5 us
    ppermute x10, waiting for transfers between devices, over_context(): return lax.ppermute(tensor, 'ctx', [(0, 1), (1, 0)])  33.7 us
    pallas_call x3, Pallas kernels, attend_back(): pl.pallas_call(attend_back_kernel, grid=(1,), out_shape=[jax.ShapeDtypeSt...  24.6 us
    ppermute x3, waiting for transfers between devices, sum_line(): got = lax.ppermute(part, 'dp', pairs)  15.1 us
    ppermute x3, starting transfers between devices, sum_line(): part = add(part, lax.ppermute(part, 'dp', pairs))  11.9 us
    ppermute x15, waiting for transfers between devices, across(): return lax.ppermute(tensor, 'fsdp', [(i, i ^ bit) for i in range(4)])  11.6 us
    ppermute x10, starting transfers between devices, over_context(): return lax.ppermute(tensor, 'ctx', [(0, 1), (1, 0)])  10.6 us
    ppermute x15, starting transfers between devices, across(): return lax.ppermute(tensor, 'fsdp', [(i, i ^ bit) for i in range(4)])  10.4 us
  transfers between devices with their start and end apart: 34, of which 14 were waited for; matrix products, arithmetic and copies ran while one was open for 6% of the time, Pallas kernels for 24%

profile of v2, /device:TPU:0, one launch (start us, length us, event | category | flops | bytes accessed | tf_op | source)
XLA Modules:
  0.0 237.0 jit_solution(4164913653626158075)
XLA Ops:
  3.4 3.0 %collective-permute-start.1 = (bf16[144,1024]{1,0:T(8,128)(2,1)S(1)}, bf16[144,1024]{1,0:T(8,128)(2,1)}, u32[]{:S(2)}, u32[]{:S(2)}) collective-permute-start(bf16[144,1024]{1,0:T(8,128)(2,1)S(1)} %concatenate.15.w_own), channel_id=1, source_target_pairs={{0,2},{1,3},{2,0},{3,1},{4,6},{5,7},{6,4},{7,5},{8,10},{9,11},{10,... | collective-permute-start | bytes 884744 | tf_op jit(solution)/shard_map/ppermute | solution.py:835
  9.2 4.3 %collective-permute-done.1.w_y = bf16[144,1024]{1,0:T(8,128)(2,1)} collective-permute-done((bf16[144,1024]{1,0:T(8,128)(2,1)S(1)}, bf16[144,1024]{1,0:T(8,128)(2,1)}, u32[]{:S(2)}, u32[]{:S(2)}) %collective-permute-start.1) | collective-permute-done | bytes 294944 | tf_op jit(solution)/shard_map/ppermute | solution.py:835
  17.0 5.5 %collective-permute-done.theirs = bf16[576,512]{1,0:T(8,128)(2,1)} collective-permute-done((bf16[576,512]{1,0:T(8,128)(2,1)S(1)}, bf16[576,512]{1,0:T(8,128)(2,1)}, u32[]{:S(2)}, u32[]{:S(2)}) %collective-permute-start) | collective-permute-done | bytes 589856 | tf_op jit(solution)/shard_map/ppermute | solution.py:839
  26.6 23.9 %attend.1 = (bf16[576,1024]{1,0:T(8,128)(2,1)}, bf16[576,1024]{1,0:T(8,128)(2,1)}, bf16[576,1024]{1,0:T(8,128)(2,1)}, f32[576,128]{1,0:T(8,128)}, bf16[960,1024]...) custom-call(s32[2]{0:T(128)} %pad_add_fusion.place, bf16[2,576,512]{2,1,0:T(8,128)(2,1)} %bitcast.85, ...), custom_call_target="tpu_custom_call" | custom-call | flops 3623878656 | bytes 10289152 | tf_op jit(solution)/shard_map/attend/pallas_call | solution.py:780
  51.9 3.1 %collective-permute-done.9.a_both = bf16[576,384]{1,0:T(8,128)(2,1)S(1)} collective-permute-done((bf16[576,384]{1,0:T(8,128)(2,1)}, bf16[576,384]{1,0:T(8,128)(2,1)S(1)}, u32[]{:S(2)}, u32[]{:S(2)}) %collective-permute-start.9) | collective-permute-done | bytes 442400 | tf_op jit(solution)/shard_map/ppermute | solution.py:835
  56.2 45.8 %feed_forward.1 = (bf16[576,512]{1,0:T(8,128)(2,1)}, bf16[576,512]{1,0:T(8,128)(2,1)}, f32[576,1024]{1,0:T(8,128)}, bf16[576,1024]{1,0:T(8,128)(2,1)}, bf16[2,2,...) custom-call(s32[2]{0:T(128)} %pad_add_fusion.place, ...), custom_call_target="tpu_custom_call" | custom-call | flops 18345885696 | bytes 21381120 | tf_op jit(solution)/shard_map/feed_forward/pallas_call | solution.py:780
  102.5 8.2 %attend_back.3 = (bf16[192,1024]{1,0:T(8,128)(2,1)}, bf16[64,1024]{1,0:T(8,128)(2,1)}, bf16[64,1024]{1,0:T(8,128)(2,1)}) custom-call(bf16[960,1024]{1,0:T(8,128)(2,1)} %get-tuple-element.99.queries_t.keys_t.values_t, bf16[960,1024]{1,0:T(8,128)(2,1)} %get-tuple-element.99.queries_t.keys_t.values_t, ...), custom_call_target="tpu_custom_call" | custom-call | flops 2013265920 | bytes 4000000 | tf_op jit(solution)/shard_map/attend_back/pallas_call | solution.py:800
  111.7 3.3 %add_convert_fusion = (bf16[1,2,72,3648]{3,2,1,0:T(8,128)(2,1)S(1)}, bf16[2,72,3648]{2,1,0:T(8,128)(2,1)}) fusion(bf16[2,2,72,3648]{3,2,1,0:T(8,128)(2,1)} %collective-permute-done.11, bf16[2,2,72,3648]{3,2,1,0:T(8,128)(2,1)S(1)} %copy-done), kind=kLoop, calls=%fused_computation.2 | loop fusion | flops 4202496 | bytes 6303744 | tf_op jit(solution)/shard_map/convert_element_type | solution.py:851
  119.3 8.3 %attend_back.4 = (bf16[192,1024]{1,0:T(8,128)(2,1)}, bf16[64,1024]{1,0:T(8,128)(2,1)}, bf16[64,1024]{1,0:T(8,128)(2,1)}) custom-call(bf16[960,1024]{1,0:T(8,128)(2,1)} %get-tuple-element.99.queries_t.keys_t.values_t, bf16[960,1024]{1,0:T(8,128)(2,1)} %get-tuple-element.99.queries_t.keys_t.values_t, ...), custom_call_target="tpu_custom_call" | custom-call | flops 2013265920 | bytes 4000000 | tf_op jit(solution)/shard_map/attend_back/pallas_call | solution.py:800
  127.6 6.1 %collective-permute-done.15 = bf16[576,512]{1,0:T(8,128)(2,1)S(1)} collective-permute-done((bf16[576,512]{1,0:T(8,128)(2,1)}, bf16[576,512]{1,0:T(8,128)(2,1)S(1)}, u32[]{:S(2)}, u32[]{:S(2)}) %collective-permute-start.15) | collective-permute-done | bytes 589856 | tf_op jit(solution)/shard_map/ppermute | solution.py:839
  133.7 8.5 %collective-permute-done.14 = bf16[2,288,384]{2,1,0:T(8,128)(2,1)} collective-permute-done((bf16[2,288,384]{2,1,0:T(8,128)(2,1)}, bf16[2,288,384]{2,1,0:T(8,128)(2,1)}, u32[]{:S(2)}, u32[]{:S(2)}) %collective-permute-start.14) | collective-permute-done | bytes 442400 | tf_op jit(solution)/shard_map/ppermute | solution.py:839
  144.6 8.1 %attend_back.5 = (bf16[192,1024]{1,0:T(8,128)(2,1)}, bf16[64,1024]{1,0:T(8,128)(2,1)}, bf16[64,1024]{1,0:T(8,128)(2,1)}) custom-call(bf16[960,1024]{1,0:T(8,128)(2,1)} %get-tuple-element.99.queries_t.keys_t.values_t, bf16[960,1024]{1,0:T(8,128)(2,1)} %get-tuple-element.99.queries_t.keys_t.values_t, ...), custom_call_target="tpu_custom_call" | custom-call | flops 2013265920 | bytes 4000000 | tf_op jit(solution)/shard_map/attend_back/pallas_call | solution.py:800
  153.6 8.7 %input_side.1 = (bf16[2,2,72,1024]{3,2,1,0:T(8,128)(2,1)}, bf16[2,2,72,1024]{3,2,1,0:T(8,128)(2,1)}, f32[576,512]{1,0:T(8,128)}, bf16[576,512]{1,0:T(8,128)(2,1)}) custom-call(s32[2]{0:T(128)} %pad_add_fusion.place, bf16[576,1024]{1,0:T(8,128)(2,1)} %get-tuple-element.71.x_seq, bf16[576,1024]{1,0:T(8,128)(2,1)} %get-tuple-element.104.normed, ...), custom_call_target="tpu_custom_call" | custom-call | flops 2415919104 | bytes 11403264 | tf_op jit(solution)/shard_map/input_side/pallas_call | solution.py:780
  163.9 2.5 %fusion.1 = bf16[2,512,576]{1,2,0:T(8,128)(2,1)} fusion(bf16[1,576,512]{2,1,0:T(8,128)(2,1)} %bitcast.84, bf16[1,576,512]{2,1,0:T(8,128)(2,1)S(1)} %bitcast.83, pred[]{:T(512)S(6)} %eq.6), kind=kLoop, calls=%fused_computation.5 | loop fusion | flops 1769472 | bytes 2359297 | tf_op jit(solution)/shard_map/transpose | solution.py:1061
  168.9 3.6 %collective-permute-start.30 = (bf16[288,384]{1,0:T(8,128)(2,1)S(1)}, bf16[288,384]{1,0:T(8,128)(2,1)S(1)}, u32[]{:S(2)}, u32[]{:S(2)}) collective-permute-start(bf16[288,384]{1,0:T(8,128)(2,1)S(1)} %fusion.10), channel_id=1, source_target_pairs={{0,8},{24,16},{1,9},{25,17},{2,10},{26,18},{3,11},{27,19},{4,12},{... | collective-permute-start | bytes 663560 | tf_op jit(solution)/shard_map/ppermute | solution.py:860
  173.8 2.9 %collective-permute-done.16 = bf16[576,512]{1,0:T(8,128)(2,1)S(1)} collective-permute-done((bf16[576,512]{1,0:T(8,128)(2,1)}, bf16[576,512]{1,0:T(8,128)(2,1)S(1)}, u32[]{:S(2)}, u32[]{:S(2)}) %collective-permute-start.16) | collective-permute-done | bytes 589856 | tf_op jit(solution)/shard_map/ppermute | solution.py:839
  183.3 4.1 %collective-permute-done.20 = bf16[2,72,1024]{2,1,0:T(8,128)(2,1)S(1)} collective-permute-done((bf16[2,72,1024]{2,1,0:T(8,128)(2,1)S(1)}, bf16[2,72,1024]{2,1,0:T(8,128)(2,1)S(1)}, u32[]{:S(2)}, u32[]{:S(2)}) %collective-permute-start.20) | collective-permute-done | bytes 294944 | tf_op jit(solution)/shard_map/ppermute | solution.py:835
  190.1 2.6 %collective-permute-done.21 = bf16[72,1024]{1,0:T(8,128)(2,1)S(1)} collective-permute-done((bf16[72,1024]{1,0:T(8,128)(2,1)S(1)}, bf16[72,1024]{1,0:T(8,128)(2,1)S(1)}, u32[]{:S(2)}, u32[]{:S(2)}) %collective-permute-start.21) | collective-permute-done | bytes 147488 | tf_op jit(solution)/shard_map/ppermute | solution.py:839
  192.8 6.9 %collective-permute-start.22 = (bf16[72,1024]{1,0:T(8,128)(2,1)S(1)}, bf16[72,1024]{1,0:T(8,128)(2,1)S(1)}, u32[]{:S(2)}, u32[]{:S(2)}) collective-permute-start(bf16[72,1024]{1,0:T(8,128)(2,1)S(1)} %fusion.15), channel_id=1, source_target_pairs={{0,8},{24,16},{1,9},{25,17},{2,10},{26,18},{3,11},{27,19},{4,12},{... | collective-permute-start | bytes 442376 | tf_op jit(solution)/shard_map/ppermute | solution.py:860
  200.4 2.0 collective-permute-done.22
  206.9 15.1 %collective-permute-done.24 = bf16[72,1024]{1,0:T(8,128)(2,1)S(1)} collective-permute-done((bf16[72,1024]{1,0:T(8,128)(2,1)S(1)}, bf16[72,1024]{1,0:T(8,128)(2,1)S(1)}, u32[]{:S(2)}, u32[]{:S(2)}) %collective-permute-start.24) | collective-permute-done | bytes 147488 | tf_op jit(solution)/shard_map/ppermute | solution.py:864
  222.5 1.8 collective-permute-start.29
  224.3 4.6 %collective-permute-done.25 = bf16[72,1024]{1,0:T(8,128)(2,1)S(1)} collective-permute-done((bf16[72,1024]{1,0:T(8,128)(2,1)S(1)}, bf16[72,1024]{1,0:T(8,128)(2,1)S(1)}, u32[]{:S(2)}, u32[]{:S(2)}) %collective-permute-start.25) | collective-permute-done | bytes 147488 | tf_op jit(solution)/shard_map/ppermute | solution.py:839
  231.3 3.4 %collective-permute-done.29 = bf16[72,3648]{1,0:T(8,128)(2,1)S(1)} collective-permute-done((bf16[72,3648]{1,0:T(8,128)(2,1)S(1)}, bf16[72,3648]{1,0:T(8,128)(2,1)S(1)}, u32[]{:S(2)}, u32[]{:S(2)}) %collective-permute-start.29) | collective-permute-done | bytes 525344 | tf_op jit(solution)/shard_map/ppermute | solution.py:839
  (134 shorter events, 49.3 us)
Async XLA Ops:
  3.4 10.1 %collective-permute-start.1 = (bf16[144,1024]{1,0:T(8,128)(2,1)S(1)}, bf16[144,1024]{1,0:T(8,128)(2,1)}, u32[]{:S(2)}, u32[]{:S(2)}) collective-permute-start(bf16[144,1024]{1,0:T(8,128)(2,1)S(1)} %concatenate.15.w_own), channel_id=1, source_target_pairs={{0,2},{1,3},{2,0},{3,1},{4,6},{5,7},{6,4},{7,5},{8,10},{9,11},{10,... | collective-permute-start | bytes 884744 | tf_op jit(solution)/shard_map/ppermute | solution.py:835
  7.6 15.0 %collective-permute-start = (bf16[576,512]{1,0:T(8,128)(2,1)S(1)}, bf16[576,512]{1,0:T(8,128)(2,1)}, u32[]{:S(2)}, u32[]{:S(2)}) collective-permute-start(bf16[576,512]{1,0:T(8,128)(2,1)S(1)} %dynamic-slice_bitcast_fusion.1), channel_id=1, source_target_pairs={{0,4},{4,0},{1,5},{5,1},{2,6},{6,2},{3,7},{7,3},{8,12},{12,8},{9,1... | collective-permute-start | bytes 1769480 | tf_op jit(solution)/shard_map/ppermute | solution.py:839
  13.6 37.0 %collective-permute-start.6 = (bf16[144,3648]{1,0:T(8,128)(2,1)S(1)}, bf16[144,3648]{1,0:T(8,128)(2,1)}, u32[]{:S(2)}, u32[]{:S(2)}) collective-permute-start(bf16[144,3648]{1,0:T(8,128)(2,1)S(1)} %pad_maximum_fusion.b_own), channel_id=1, source_target_pairs={{0,1},{1,0},{2,3},{3,2},{4,5},{5,4},{6,7},{7,6},{8,9},{9,8},{10,11... | collective-permute-start | bytes 3151880 | tf_op jit(solution)/shard_map/ppermute | solution.py:835
  13.6 37.0 %collective-permute-start.4 = (bf16[144,3648]{1,0:T(8,128)(2,1)S(1)}, bf16[144,3648]{1,0:T(8,128)(2,1)}, u32[]{:S(2)}, u32[]{:S(2)}) collective-permute-start(bf16[144,3648]{1,0:T(8,128)(2,1)S(1)} %pad_maximum_fusion.b_own), channel_id=1, source_target_pairs={{0,2},{1,3},{2,0},{3,1},{4,6},{5,7},{6,4},{7,5},{8,10},{9,11},{10,... | collective-permute-start | bytes 3151880 | tf_op jit(solution)/shard_map/ppermute | solution.py:835
  15.3 9.9 %collective-permute-start.2 = (bf16[144,1024]{1,0:T(8,128)(2,1)S(1)}, bf16[144,1024]{1,0:T(8,128)(2,1)}, u32[]{:S(2)}, u32[]{:S(2)}) collective-permute-start(bf16[144,1024]{1,0:T(8,128)(2,1)S(1)} %concatenate.15.w_own), channel_id=1, source_target_pairs={{0,1},{1,0},{2,3},{3,2},{4,5},{5,4},{6,7},{7,6},{8,9},{9,8},{10,11... | collective-permute-start | bytes 884744 | tf_op jit(solution)/shard_map/ppermute | solution.py:835
  22.5 28.1 %collective-permute-start.8 = (bf16[576,512]{1,0:T(8,128)(2,1)S(1)}, bf16[576,512]{1,0:T(8,128)(2,1)S(1)}, u32[]{:S(2)}, u32[]{:S(2)}) collective-permute-start(bf16[576,512]{1,0:T(8,128)(2,1)S(1)} %dynamic-slice_bitcast_fusion), channel_id=1, source_target_pairs={{0,4},{4,0},{1,5},{5,1},{2,6},{6,2},{3,7},{7,3},{8,12},{12,8},{9,1... | collective-permute-start | bytes 1769480 | tf_op jit(solution)/shard_map/ppermute | solution.py:839
  25.3 25.3 %collective-permute-start.7 = (bf16[576,384]{1,0:T(8,128)(2,1)S(1)}, bf16[576,384]{1,0:T(8,128)(2,1)S(1)}, u32[]{:S(2)}, u32[]{:S(2)}) collective-permute-start(bf16[576,384]{1,0:T(8,128)(2,1)S(1)} %bitcast.88), channel_id=1, source_target_pairs={{0,1},{1,0},{2,3},{3,2},{4,5},{5,4},{6,7},{7,6},{8,9},{9,8},{10,11... | collective-permute-start | bytes 1327112 | tf_op jit(solution)/shard_map/ppermute | solution.py:835
  25.3 25.3 %collective-permute-start.5 = (bf16[576,384]{1,0:T(8,128)(2,1)S(1)}, bf16[576,384]{1,0:T(8,128)(2,1)S(1)}, u32[]{:S(2)}, u32[]{:S(2)}) collective-permute-start(bf16[576,384]{1,0:T(8,128)(2,1)S(1)} %bitcast.89), channel_id=1, source_target_pairs={{0,2},{1,3},{2,0},{3,1},{4,6},{5,7},{6,4},{7,5},{8,10},{9,11},{10,... | collective-permute-start | bytes 1327112 | tf_op jit(solution)/shard_map/ppermute | solution.py:835
  102.0 8.7 %collective-permute-start.11 = (bf16[2,2,72,3648]{3,2,1,0:T(8,128)(2,1)}, bf16[2,2,72,3648]{3,2,1,0:T(8,128)(2,1)}, u32[]{:S(2)}, u32[]{:S(2)}) collective-permute-start(bf16[2,2,72,3648]{3,2,1,0:T(8,128)(2,1)} %get-tuple-element.85), channel_id=1, source_target_pairs={{0,1},{1,0},{2,3},{3,2},{4,5},{5,4},{6,7},{7,6},{8,9},{9,8},{10,11... | collective-permute-start | bytes 6303752 | tf_op jit(solution)/shard_map/ppermute | solution.py:835
  116.0 26.2 %collective-permute-start.13 = (bf16[2,72,3648]{2,1,0:T(8,128)(2,1)}, bf16[2,72,3648]{2,1,0:T(8,128)(2,1)S(1)}, u32[]{:S(2)}, u32[]{:S(2)}) collective-permute-start(bf16[2,72,3648]{2,1,0:T(8,128)(2,1)} %get-tuple-element.96), channel_id=1, source_target_pairs={{0,2},{1,3},{2,0},{3,1},{4,6},{5,7},{6,4},{7,5},{8,10},{9,11},{10,... | collective-permute-start | bytes 3151880 | tf_op jit(solution)/shard_map/ppermute | solution.py:835
  117.3 16.4 %collective-permute-start.15 = (bf16[576,512]{1,0:T(8,128)(2,1)}, bf16[576,512]{1,0:T(8,128)(2,1)S(1)}, u32[]{:S(2)}, u32[]{:S(2)}) collective-permute-start(bf16[576,512]{1,0:T(8,128)(2,1)} %get-tuple-element.98), channel_id=1, source_target_pairs={{0,4},{4,0},{1,5},{5,1},{2,6},{6,2},{3,7},{7,3},{8,12},{12,8},{9,1... | collective-permute-start | bytes 1769480 | tf_op jit(solution)/shard_map/ppermute | solution.py:839
  117.8 24.4 %collective-permute-start.14 = (bf16[2,288,384]{2,1,0:T(8,128)(2,1)}, bf16[2,288,384]{2,1,0:T(8,128)(2,1)}, u32[]{:S(2)}, u32[]{:S(2)}) collective-permute-start(bf16[2,288,384]{2,1,0:T(8,128)(2,1)} %get-tuple-element.97), channel_id=1, source_target_pairs={{0,4},{4,0},{1,5},{5,1},{2,6},{6,2},{3,7},{7,3},{8,12},{12,8},{9,1... | collective-permute-start | bytes 1327112 | tf_op jit(solution)/shard_map/ppermute | solution.py:839
  144.0 22.4 %collective-permute-start.17 = (bf16[72,3648]{1,0:T(8,128)(2,1)S(1)}, bf16[72,3648]{1,0:T(8,128)(2,1)}, u32[]{:S(2)}, u32[]{:S(2)}) collective-permute-start(bf16[72,3648]{1,0:T(8,128)(2,1)S(1)} %fusion.6), channel_id=1, source_target_pairs={{0,4},{4,0},{1,5},{5,1},{2,6},{6,2},{3,7},{7,3},{8,12},{12,8},{9,1... | collective-permute-start | bytes 1575944 | tf_op jit(solution)/shard_map/ppermute | solution.py:839
  152.7 13.8 %collective-permute-start.18 = (bf16[288,384]{1,0:T(8,128)(2,1)}, bf16[288,384]{1,0:T(8,128)(2,1)S(1)}, u32[]{:S(2)}, u32[]{:S(2)}) collective-permute-start(bf16[288,384]{1,0:T(8,128)(2,1)} %fusion.17), channel_id=1, source_target_pairs={{0,2},{1,3},{2,0},{3,1},{4,6},{5,7},{6,4},{7,5},{8,10},{9,11},{10,... | collective-permute-start | bytes 663560 | tf_op jit(solution)/shard_map/ppermute | solution.py:835
  162.4 14.4 %collective-permute-start.16 = (bf16[576,512]{1,0:T(8,128)(2,1)}, bf16[576,512]{1,0:T(8,128)(2,1)S(1)}, u32[]{:S(2)}, u32[]{:S(2)}) collective-permute-start(bf16[576,512]{1,0:T(8,128)(2,1)} %get-tuple-element.123), channel_id=1, source_target_pairs={{0,4},{4,0},{1,5},{5,1},{2,6},{6,2},{3,7},{7,3},{8,12},{12,8},{9,1... | collective-permute-start | bytes 1769480 | tf_op jit(solution)/shard_map/ppermute | solution.py:839
  167.7 11.2 %collective-permute-start.19 = (bf16[2,2,72,1024]{3,2,1,0:T(8,128)(2,1)S(1)}, bf16[2,2,72,1024]{3,2,1,0:T(8,128)(2,1)S(1)}, u32[]{:S(2)}, u32[]{:S(2)}) collective-permute-start(bf16[2,2,72,1024]{3,2,1,0:T(8,128)(2,1)S(1)} %copy-done.15), channel_id=1, source_target_pairs={{0,1},{1,0},{2,3},{3,2},{4,5},{5,4},{6,7},{7,6},{8,9},{9,8},{10,11... | collective-permute-start | bytes 1769480 | tf_op jit(solution)/shard_map/ppermute | solution.py:835
  168.9 9.3 %collective-permute-start.30 = (bf16[288,384]{1,0:T(8,128)(2,1)S(1)}, bf16[288,384]{1,0:T(8,128)(2,1)S(1)}, u32[]{:S(2)}, u32[]{:S(2)}) collective-permute-start(bf16[288,384]{1,0:T(8,128)(2,1)S(1)} %fusion.10), channel_id=1, source_target_pairs={{0,8},{24,16},{1,9},{25,17},{2,10},{26,18},{3,11},{27,19},{4,12},{... | collective-permute-start | bytes 663560 | tf_op jit(solution)/shard_map/ppermute | solution.py:860
  172.5 16.8 %collective-permute-start.26 = (bf16[72,3648]{1,0:T(8,128)(2,1)S(1)}, bf16[72,3648]{1,0:T(8,128)(2,1)S(1)}, u32[]{:S(2)}, u32[]{:S(2)}) collective-permute-start(bf16[72,3648]{1,0:T(8,128)(2,1)S(1)} %fusion.3), channel_id=1, source_target_pairs={{0,8},{24,16},{1,9},{25,17},{2,10},{26,18},{3,11},{27,19},{4,12},{... | collective-permute-start | bytes 1575944 | tf_op jit(solution)/shard_map/ppermute | solution.py:860
  182.0 17.7 %collective-permute-start.32 = (bf16[288,384]{1,0:T(8,128)(2,1)S(1)}, bf16[288,384]{1,0:T(8,128)(2,1)S(1)}, u32[]{:S(2)}, u32[]{:S(2)}) collective-permute-start(bf16[288,384]{1,0:T(8,128)(2,1)S(1)} %add_convert_fusion.8), channel_id=1, source_target_pairs={{8,0},{16,24},{9,1},{17,25},{10,2},{18,26},{11,3},{19,27},{12,4},{... | collective-permute-start | bytes 663560 | tf_op jit(solution)/shard_map/ppermute | solution.py:864
  189.4 13.7 %collective-permute-start.27 = (bf16[72,3648]{1,0:T(8,128)(2,1)S(1)}, bf16[72,3648]{1,0:T(8,128)(2,1)S(1)}, u32[]{:S(2)}, u32[]{:S(2)}) collective-permute-start(bf16[72,3648]{1,0:T(8,128)(2,1)S(1)} %add_convert_fusion.3), channel_id=1, source_target_pairs={{8,16},{16,8},{9,17},{17,9},{10,18},{18,10},{11,19},{19,11},{12,20... | collective-permute-start | bytes 1575944 | tf_op jit(solution)/shard_map/ppermute | solution.py:861
  192.8 9.6 %collective-permute-start.22 = (bf16[72,1024]{1,0:T(8,128)(2,1)S(1)}, bf16[72,1024]{1,0:T(8,128)(2,1)S(1)}, u32[]{:S(2)}, u32[]{:S(2)}) collective-permute-start(bf16[72,1024]{1,0:T(8,128)(2,1)S(1)} %fusion.15), channel_id=1, source_target_pairs={{0,8},{24,16},{1,9},{25,17},{2,10},{26,18},{3,11},{27,19},{4,12},{... | collective-permute-start | bytes 442376 | tf_op jit(solution)/shard_map/ppermute | solution.py:860
  203.2 19.2 %collective-permute-start.28 = (bf16[72,3648]{1,0:T(8,128)(2,1)S(1)}, bf16[72,3648]{1,0:T(8,128)(2,1)S(1)}, u32[]{:S(2)}, u32[]{:S(2)}) collective-permute-start(bf16[72,3648]{1,0:T(8,128)(2,1)S(1)} %add_convert_fusion.2), channel_id=1, source_target_pairs={{8,0},{16,24},{9,1},{17,25},{10,2},{18,26},{11,3},{19,27},{12,4},{... | collective-permute-start | bytes 1575944 | tf_op jit(solution)/shard_map/ppermute | solution.py:864
  204.6 17.5 %collective-permute-start.24 = (bf16[72,1024]{1,0:T(8,128)(2,1)S(1)}, bf16[72,1024]{1,0:T(8,128)(2,1)S(1)}, u32[]{:S(2)}, u32[]{:S(2)}) collective-permute-start(bf16[72,1024]{1,0:T(8,128)(2,1)S(1)} %add_convert_fusion.10), channel_id=1, source_target_pairs={{8,0},{16,24},{9,1},{17,25},{10,2},{18,26},{11,3},{19,27},{12,4},{... | collective-permute-start | bytes 442376 | tf_op jit(solution)/shard_map/ppermute | solution.py:864
  222.5 12.2 %collective-permute-start.29 = (bf16[72,3648]{1,0:T(8,128)(2,1)S(1)}, bf16[72,3648]{1,0:T(8,128)(2,1)S(1)}, u32[]{:S(2)}, u32[]{:S(2)}) collective-permute-start(bf16[72,3648]{1,0:T(8,128)(2,1)S(1)} %broadcast_select_fusion), channel_id=1, source_target_pairs={{0,4},{4,0},{1,5},{5,1},{2,6},{6,2},{3,7},{7,3},{8,12},{12,8},{9,1... | collective-permute-start | bytes 1575944 | tf_op jit(solution)/shard_map/ppermute | solution.py:839
  (31 other events, 224.0 us)
